TPU v7x, 256 devices: a whole 4x4x8 slice. The times are simulated.
256 devices in a mesh: dp: 8 (over y, x_lo), ctx: 32 (over z, x_hi, core).
Axes of the slice: x: 4 (x_hi: 2, x_lo: 2; x = x_hi * 2 + x_lo), y: 4, z: 8, core: 2. Of those that a mesh axis runs over, the one named last changes fastest.
Arguments:
- query: bfloat16 [32768, 2048], P(('dp', 'ctx')), parts along dimension 0, may hold values from -128 to 128
- keys: bfloat16 [32768, 256], P(('dp', 'ctx')), parts along dimension 0, may hold values from -8 to 8
- values: bfloat16 [32768, 256], P(('dp', 'ctx')), parts along dimension 0, may hold values from -6 to 6
- attn_out: bfloat16 [32768, 2048], P(('dp', 'ctx')), parts along dimension 0, may hold values from -2 to 2
- grad_out: bfloat16 [32768, 2048], P(('dp', 'ctx')), parts along dimension 0, may hold values from -6 to 6
- log_total: float32 [16, 32768], P(None, ('dp', 'ctx')), parts along dimension 1, as said below
- doc_lengths: int32 [128], P('dp'), parts along dimension 0, may hold values from 1 to 1024, as said below
- block_order: int32 [512], P('dp'), parts along dimension 0, may hold values from 0 to 63, as said below
Outputs:
- query_grad: bfloat16 [32768, 2048], P(('dp', 'ctx')), parts along dimension 0
- key_grad: bfloat16 [32768, 256], P(('dp', 'ctx')), parts along dimension 0
- value_grad: bfloat16 [32768, 256], P(('dp', 'ctx')), parts along dimension 0
There are 8 independent parts, one for each index of `dp`. A program takes and returns all parts, laid end to end along the dimension named above; each array names one. Nothing has to cross between parts.
Inputs may be any that keep to these rules, and one draw needn't show every extreme that they name: `doc_lengths`: 16 document lengths of at least 1 that add up to 4096; the largest is exactly 1024. `block_order`: each of the 64 blocks of 64 positions once. log_total[h, i] is the log of the sum over j with visible(i, j) = 1 of exp(score[h, i, j]).
All inputs are finite; a program needn't handle non-finite values.
Results may differ from a plain program's by a relative error of at most 0.011.
Values may be sent and summed in bfloat16 or wider, within the bound.
A program may use at most 64 MiB of HBM per device.

v0:
```python
import jax
import jax.numpy as jnp
from jax import lax
from jax.sharding import PartitionSpec as P

HD = 128
GROUP_Q = 8
KV_GROUPS = 2


def passed_along(value, axis, steps):
    count = lax.axis_size(axis)
    pairs = [(source, (source + steps) % count) for source in range(count)]
    return lax.ppermute(value, axis, pairs)


def token_numbers(block_order, row_start, length, half_rows):
    local_ids = row_start + jnp.arange(length, dtype=jnp.int32)
    slot_ids = jnp.arange(block_order.shape[0], dtype=jnp.int32)
    onehot = ((local_ids // half_rows)[:, None] == slot_ids[None, :]).astype(jnp.int32)
    return jnp.sum(onehot * block_order[None, :], axis=1) * half_rows + local_ids % half_rows


def document_numbers(doc_ends, tok_here):
    return jnp.sum((doc_ends[None, :] <= tok_here[:, None]).astype(jnp.int32), axis=1)


def local(query, keys, values, attn_out, grad_out, log_total, doc_lengths, block_order):
    devices = lax.axis_size("ctx")
    my_index = lax.axis_index("ctx")
    local_rows = query.shape[0]
    half_rows = local_rows // 2
    inv_root = HD ** (-0.5)
    doc_ends = jnp.cumsum(doc_lengths)
    tok_q = token_numbers(block_order, my_index * local_rows, local_rows, half_rows)
    doc_q = document_numbers(doc_ends, tok_q)
    query_heads = query.reshape(local_rows, KV_GROUPS, GROUP_Q, HD)
    dout_heads = grad_out.reshape(local_rows, KV_GROUPS, GROUP_Q, HD)
    output_heads = attn_out.reshape(local_rows, KV_GROUPS, GROUP_Q, HD)
    lse_heads = log_total.reshape(KV_GROUPS, GROUP_Q, local_rows)
    row_delta = jnp.einsum(
        "igqd,igqd->gqi", dout_heads, output_heads, preferred_element_type=jnp.float32
    )

    def visible(row_start, length):
        tok_k = token_numbers(block_order, row_start, length, half_rows)
        doc_k = document_numbers(doc_ends, tok_k)
        return (doc_q[:, None] == doc_k[None, :]) & (tok_k[None, :] <= tok_q[:, None])

    def contribute(kv_piece, row_start):
        length = kv_piece.shape[1]
        allowed = visible(row_start, length)
        key_heads = kv_piece[0].reshape(length, KV_GROUPS, HD)
        value_heads = kv_piece[1].reshape(length, KV_GROUPS, HD)
        scores = (
            jnp.einsum("igqd,jgd->gqij", query_heads, key_heads, preferred_element_type=jnp.float32)
            * inv_root
        )
        safe = jnp.where(allowed, scores - lse_heads[..., None], 0.0)
        probs = jnp.where(allowed, jnp.exp(safe), 0.0)
        probs_low = probs.astype(jnp.bfloat16)
        dprobs = jnp.einsum(
            "igqd,jgd->gqij", dout_heads, value_heads, preferred_element_type=jnp.float32
        )
        dscore = (probs * (dprobs - row_delta[..., None])).astype(jnp.bfloat16)
        query_part = (
            jnp.einsum("gqij,jgd->igqd", dscore, key_heads, preferred_element_type=jnp.float32)
            * inv_root
        )
        key_part = (
            jnp.einsum("gqij,igqd->jgd", dscore, query_heads, preferred_element_type=jnp.float32)
            * inv_root
        )
        value_part = jnp.einsum(
            "gqij,igqd->jgd", probs_low, dout_heads, preferred_element_type=jnp.float32
        )
        return (query_part, key_part, value_part)

    query_zero = jnp.zeros((local_rows, KV_GROUPS, GROUP_Q, HD), jnp.float32)
    kv_pair = jnp.stack([keys, values])
    grad_zero = jnp.zeros((2, local_rows, KV_GROUPS, HD), jnp.float32)

    def circle_step(step_index, carried):
        kv_now, grad_now, query_acc = carried
        owner = (my_index - step_index) % devices
        query_part, key_part, value_part = contribute(kv_now, owner * local_rows)
        grad_now = grad_now + jnp.stack([key_part, value_part])
        kv_now = passed_along(kv_now, "ctx", 1)
        grad_now = passed_along(grad_now, "ctx", 1)
        return (kv_now, grad_now, query_acc + query_part)

    kv_end, grad_pair, query_acc = lax.fori_loop(
        0, devices, circle_step, (kv_pair, grad_zero, query_zero)
    )
    key_acc = grad_pair[0]
    value_acc = grad_pair[1]
    query_grad = query_acc.reshape(local_rows, KV_GROUPS * GROUP_Q * HD).astype(jnp.bfloat16)
    key_grad = key_acc.reshape(local_rows, KV_GROUPS * HD).astype(jnp.bfloat16)
    value_grad = value_acc.reshape(local_rows, KV_GROUPS * HD).astype(jnp.bfloat16)
    return (query_grad, key_grad, value_grad)


def solution(mesh):
    return jax.shard_map(
        local,
        mesh=mesh,
        in_specs=(
            P(("dp", "ctx"), None),
            P(("dp", "ctx"), None),
            P(("dp", "ctx"), None),
            P(("dp", "ctx"), None),
            P(("dp", "ctx"), None),
            P(None, ("dp", "ctx")),
            P("dp"),
            P("dp"),
        ),
        out_specs=(P(("dp", "ctx"), None), P(("dp", "ctx"), None), P(("dp", "ctx"), None)),
        check_vma=False,
    )
```

profile of v0, /device:TPU:1, one launch (start us, length us, event | category | flops | bytes accessed | tf_op | source)
XLA Modules:
  0.0 371.2 jit_solution(7093114789490363977)
XLA Ops:
  8.9 360.1 %while.21 = (s32[]{:T(128)}, bf16[2,128,256]{1,2,0:T(8,128)(2,1)S(1)}, f32[2,128,2,128]{3,1,2,0:T(8,128)S(1)}, f32[128,2,8,128]{3,0,2,1:T(8,128)S(1)}, s32[128]{...) while((s32[]{:T(128)}, ...), condition=%wide.region_6.7_spmd.clone, body=%wide.region_3.6_spmd.clone.sunk | while | flops 338675200 | bytes 12310732 | solution.py:92
  63.9 6.8 %collective-permute-done = bf16[2,128,256]{1,2,0:T(8,128)(2,1)S(1)} collective-permute-done((bf16[2,128,256]{1,2,0:T(8,128)(2,1)S(1)}, bf16[2,128,256]{1,2,0:T(8,128)(2,1)S(1)}, u32[]{:S(2)}, u32[]{:S(2)}) %collective-permute-start) | collective-permute-done | bytes 131104 | tf_op jit(solution)/shard_map/while/body/eval_jaxpr/ppermute | solution.py:14
  75.2 6.8 %collective-permute-done = bf16[2,128,256]{1,2,0:T(8,128)(2,1)S(1)} collective-permute-done((bf16[2,128,256]{1,2,0:T(8,128)(2,1)S(1)}, bf16[2,128,256]{1,2,0:T(8,128)(2,1)S(1)}, u32[]{:S(2)}, u32[]{:S(2)}) %collective-permute-start) | collective-permute-done | bytes 131104 | tf_op jit(solution)/shard_map/while/body/eval_jaxpr/ppermute | solution.py:14
  86.6 6.8 %collective-permute-done = bf16[2,128,256]{1,2,0:T(8,128)(2,1)S(1)} collective-permute-done((bf16[2,128,256]{1,2,0:T(8,128)(2,1)S(1)}, bf16[2,128,256]{1,2,0:T(8,128)(2,1)S(1)}, u32[]{:S(2)}, u32[]{:S(2)}) %collective-permute-start) | collective-permute-done | bytes 131104 | tf_op jit(solution)/shard_map/while/body/eval_jaxpr/ppermute | solution.py:14
  98.0 6.8 %collective-permute-done = bf16[2,128,256]{1,2,0:T(8,128)(2,1)S(1)} collective-permute-done((bf16[2,128,256]{1,2,0:T(8,128)(2,1)S(1)}, bf16[2,128,256]{1,2,0:T(8,128)(2,1)S(1)}, u32[]{:S(2)}, u32[]{:S(2)}) %collective-permute-start) | collective-permute-done | bytes 131104 | tf_op jit(solution)/shard_map/while/body/eval_jaxpr/ppermute | solution.py:14
  109.4 6.8 %collective-permute-done = bf16[2,128,256]{1,2,0:T(8,128)(2,1)S(1)} collective-permute-done((bf16[2,128,256]{1,2,0:T(8,128)(2,1)S(1)}, bf16[2,128,256]{1,2,0:T(8,128)(2,1)S(1)}, u32[]{:S(2)}, u32[]{:S(2)}) %collective-permute-start) | collective-permute-done | bytes 131104 | tf_op jit(solution)/shard_map/while/body/eval_jaxpr/ppermute | solution.py:14
  120.8 6.8 %collective-permute-done = bf16[2,128,256]{1,2,0:T(8,128)(2,1)S(1)} collective-permute-done((bf16[2,128,256]{1,2,0:T(8,128)(2,1)S(1)}, bf16[2,128,256]{1,2,0:T(8,128)(2,1)S(1)}, u32[]{:S(2)}, u32[]{:S(2)}) %collective-permute-start) | collective-permute-done | bytes 131104 | tf_op jit(solution)/shard_map/while/body/eval_jaxpr/ppermute | solution.py:14
  132.2 6.8 %collective-permute-done = bf16[2,128,256]{1,2,0:T(8,128)(2,1)S(1)} collective-permute-done((bf16[2,128,256]{1,2,0:T(8,128)(2,1)S(1)}, bf16[2,128,256]{1,2,0:T(8,128)(2,1)S(1)}, u32[]{:S(2)}, u32[]{:S(2)}) %collective-permute-start) | collective-permute-done | bytes 131104 | tf_op jit(solution)/shard_map/while/body/eval_jaxpr/ppermute | solution.py:14
  143.6 6.8 %collective-permute-done = bf16[2,128,256]{1,2,0:T(8,128)(2,1)S(1)} collective-permute-done((bf16[2,128,256]{1,2,0:T(8,128)(2,1)S(1)}, bf16[2,128,256]{1,2,0:T(8,128)(2,1)S(1)}, u32[]{:S(2)}, u32[]{:S(2)}) %collective-permute-start) | collective-permute-done | bytes 131104 | tf_op jit(solution)/shard_map/while/body/eval_jaxpr/ppermute | solution.py:14
  155.0 6.8 %collective-permute-done = bf16[2,128,256]{1,2,0:T(8,128)(2,1)S(1)} collective-permute-done((bf16[2,128,256]{1,2,0:T(8,128)(2,1)S(1)}, bf16[2,128,256]{1,2,0:T(8,128)(2,1)S(1)}, u32[]{:S(2)}, u32[]{:S(2)}) %collective-permute-start) | collective-permute-done | bytes 131104 | tf_op jit(solution)/shard_map/while/body/eval_jaxpr/ppermute | solution.py:14
  166.4 6.8 %collective-permute-done = bf16[2,128,256]{1,2,0:T(8,128)(2,1)S(1)} collective-permute-done((bf16[2,128,256]{1,2,0:T(8,128)(2,1)S(1)}, bf16[2,128,256]{1,2,0:T(8,128)(2,1)S(1)}, u32[]{:S(2)}, u32[]{:S(2)}) %collective-permute-start) | collective-permute-done | bytes 131104 | tf_op jit(solution)/shard_map/while/body/eval_jaxpr/ppermute | solution.py:14
  177.8 6.8 %collective-permute-done = bf16[2,128,256]{1,2,0:T(8,128)(2,1)S(1)} collective-permute-done((bf16[2,128,256]{1,2,0:T(8,128)(2,1)S(1)}, bf16[2,128,256]{1,2,0:T(8,128)(2,1)S(1)}, u32[]{:S(2)}, u32[]{:S(2)}) %collective-permute-start) | collective-permute-done | bytes 131104 | tf_op jit(solution)/shard_map/while/body/eval_jaxpr/ppermute | solution.py:14
  189.2 6.8 %collective-permute-done = bf16[2,128,256]{1,2,0:T(8,128)(2,1)S(1)} collective-permute-done((bf16[2,128,256]{1,2,0:T(8,128)(2,1)S(1)}, bf16[2,128,256]{1,2,0:T(8,128)(2,1)S(1)}, u32[]{:S(2)}, u32[]{:S(2)}) %collective-permute-start) | collective-permute-done | bytes 131104 | tf_op jit(solution)/shard_map/while/body/eval_jaxpr/ppermute | solution.py:14
  200.6 6.8 %collective-permute-done = bf16[2,128,256]{1,2,0:T(8,128)(2,1)S(1)} collective-permute-done((bf16[2,128,256]{1,2,0:T(8,128)(2,1)S(1)}, bf16[2,128,256]{1,2,0:T(8,128)(2,1)S(1)}, u32[]{:S(2)}, u32[]{:S(2)}) %collective-permute-start) | collective-permute-done | bytes 131104 | tf_op jit(solution)/shard_map/while/body/eval_jaxpr/ppermute | solution.py:14
  212.0 6.8 %collective-permute-done = bf16[2,128,256]{1,2,0:T(8,128)(2,1)S(1)} collective-permute-done((bf16[2,128,256]{1,2,0:T(8,128)(2,1)S(1)}, bf16[2,128,256]{1,2,0:T(8,128)(2,1)S(1)}, u32[]{:S(2)}, u32[]{:S(2)}) %collective-permute-start) | collective-permute-done | bytes 131104 | tf_op jit(solution)/shard_map/while/body/eval_jaxpr/ppermute | solution.py:14
  223.4 6.8 %collective-permute-done = bf16[2,128,256]{1,2,0:T(8,128)(2,1)S(1)} collective-permute-done((bf16[2,128,256]{1,2,0:T(8,128)(2,1)S(1)}, bf16[2,128,256]{1,2,0:T(8,128)(2,1)S(1)}, u32[]{:S(2)}, u32[]{:S(2)}) %collective-permute-start) | collective-permute-done | bytes 131104 | tf_op jit(solution)/shard_map/while/body/eval_jaxpr/ppermute | solution.py:14
  234.8 6.8 %collective-permute-done = bf16[2,128,256]{1,2,0:T(8,128)(2,1)S(1)} collective-permute-done((bf16[2,128,256]{1,2,0:T(8,128)(2,1)S(1)}, bf16[2,128,256]{1,2,0:T(8,128)(2,1)S(1)}, u32[]{:S(2)}, u32[]{:S(2)}) %collective-permute-start) | collective-permute-done | bytes 131104 | tf_op jit(solution)/shard_map/while/body/eval_jaxpr/ppermute | solution.py:14
  246.2 6.8 %collective-permute-done = bf16[2,128,256]{1,2,0:T(8,128)(2,1)S(1)} collective-permute-done((bf16[2,128,256]{1,2,0:T(8,128)(2,1)S(1)}, bf16[2,128,256]{1,2,0:T(8,128)(2,1)S(1)}, u32[]{:S(2)}, u32[]{:S(2)}) %collective-permute-start) | collective-permute-done | bytes 131104 | tf_op jit(solution)/shard_map/while/body/eval_jaxpr/ppermute | solution.py:14
  257.5 6.8 %collective-permute-done = bf16[2,128,256]{1,2,0:T(8,128)(2,1)S(1)} collective-permute-done((bf16[2,128,256]{1,2,0:T(8,128)(2,1)S(1)}, bf16[2,128,256]{1,2,0:T(8,128)(2,1)S(1)}, u32[]{:S(2)}, u32[]{:S(2)}) %collective-permute-start) | collective-permute-done | bytes 131104 | tf_op jit(solution)/shard_map/while/body/eval_jaxpr/ppermute | solution.py:14
  268.9 6.8 %collective-permute-done = bf16[2,128,256]{1,2,0:T(8,128)(2,1)S(1)} collective-permute-done((bf16[2,128,256]{1,2,0:T(8,128)(2,1)S(1)}, bf16[2,128,256]{1,2,0:T(8,128)(2,1)S(1)}, u32[]{:S(2)}, u32[]{:S(2)}) %collective-permute-start) | collective-permute-done | bytes 131104 | tf_op jit(solution)/shard_map/while/body/eval_jaxpr/ppermute | solution.py:14
  280.3 6.8 %collective-permute-done = bf16[2,128,256]{1,2,0:T(8,128)(2,1)S(1)} collective-permute-done((bf16[2,128,256]{1,2,0:T(8,128)(2,1)S(1)}, bf16[2,128,256]{1,2,0:T(8,128)(2,1)S(1)}, u32[]{:S(2)}, u32[]{:S(2)}) %collective-permute-start) | collective-permute-done | bytes 131104 | tf_op jit(solution)/shard_map/while/body/eval_jaxpr/ppermute | solution.py:14
  291.7 6.8 %collective-permute-done = bf16[2,128,256]{1,2,0:T(8,128)(2,1)S(1)} collective-permute-done((bf16[2,128,256]{1,2,0:T(8,128)(2,1)S(1)}, bf16[2,128,256]{1,2,0:T(8,128)(2,1)S(1)}, u32[]{:S(2)}, u32[]{:S(2)}) %collective-permute-start) | collective-permute-done | bytes 131104 | tf_op jit(solution)/shard_map/while/body/eval_jaxpr/ppermute | solution.py:14
  303.1 6.8 %collective-permute-done = bf16[2,128,256]{1,2,0:T(8,128)(2,1)S(1)} collective-permute-done((bf16[2,128,256]{1,2,0:T(8,128)(2,1)S(1)}, bf16[2,128,256]{1,2,0:T(8,128)(2,1)S(1)}, u32[]{:S(2)}, u32[]{:S(2)}) %collective-permute-start) | collective-permute-done | bytes 131104 | tf_op jit(solution)/shard_map/while/body/eval_jaxpr/ppermute | solution.py:14
  325.9 6.8 %collective-permute-done = bf16[2,128,256]{1,2,0:T(8,128)(2,1)S(1)} collective-permute-done((bf16[2,128,256]{1,2,0:T(8,128)(2,1)S(1)}, bf16[2,128,256]{1,2,0:T(8,128)(2,1)S(1)}, u32[]{:S(2)}, u32[]{:S(2)}) %collective-permute-start) | collective-permute-done | bytes 131104 | tf_op jit(solution)/shard_map/while/body/eval_jaxpr/ppermute | solution.py:14
  (559 shorter events, 210.0 us)
Async XLA Ops:
  63.3 9.5 %collective-permute-start.1 = (f32[2,128,2,128]{3,1,2,0:T(8,128)S(1)}, f32[2,128,2,128]{3,1,2,0:T(8,128)S(1)}, u32[]{:S(2)}, u32[]{:S(2)}) collective-permute-start(f32[2,128,2,128]{3,1,2,0:T(8,128)S(1)} %maximum_add_fusion.2), channel_id=1, source_target_pairs={{0,1},{1,2},{2,3},{3,4},{4,5},{5,6},{6,7},{7,8},{8,9},{9,10},{10,1... | collective-permute-start | bytes 786440 | tf_op jit(solution)/shard_map/while/body/eval_jaxpr/ppermute | solution.py:14
  74.7 9.5 %collective-permute-start.1 = (f32[2,128,2,128]{3,1,2,0:T(8,128)S(1)}, f32[2,128,2,128]{3,1,2,0:T(8,128)S(1)}, u32[]{:S(2)}, u32[]{:S(2)}) collective-permute-start(f32[2,128,2,128]{3,1,2,0:T(8,128)S(1)} %maximum_add_fusion.2), channel_id=1, source_target_pairs={{0,1},{1,2},{2,3},{3,4},{4,5},{5,6},{6,7},{7,8},{8,9},{9,10},{10,1... | collective-permute-start | bytes 786440 | tf_op jit(solution)/shard_map/while/body/eval_jaxpr/ppermute | solution.py:14
  86.1 9.5 %collective-permute-start.1 = (f32[2,128,2,128]{3,1,2,0:T(8,128)S(1)}, f32[2,128,2,128]{3,1,2,0:T(8,128)S(1)}, u32[]{:S(2)}, u32[]{:S(2)}) collective-permute-start(f32[2,128,2,128]{3,1,2,0:T(8,128)S(1)} %maximum_add_fusion.2), channel_id=1, source_target_pairs={{0,1},{1,2},{2,3},{3,4},{4,5},{5,6},{6,7},{7,8},{8,9},{9,10},{10,1... | collective-permute-start | bytes 786440 | tf_op jit(solution)/shard_map/while/body/eval_jaxpr/ppermute | solution.py:14
  97.4 9.5 %collective-permute-start.1 = (f32[2,128,2,128]{3,1,2,0:T(8,128)S(1)}, f32[2,128,2,128]{3,1,2,0:T(8,128)S(1)}, u32[]{:S(2)}, u32[]{:S(2)}) collective-permute-start(f32[2,128,2,128]{3,1,2,0:T(8,128)S(1)} %maximum_add_fusion.2), channel_id=1, source_target_pairs={{0,1},{1,2},{2,3},{3,4},{4,5},{5,6},{6,7},{7,8},{8,9},{9,10},{10,1... | collective-permute-start | bytes 786440 | tf_op jit(solution)/shard_map/while/body/eval_jaxpr/ppermute | solution.py:14
  108.8 9.5 %collective-permute-start.1 = (f32[2,128,2,128]{3,1,2,0:T(8,128)S(1)}, f32[2,128,2,128]{3,1,2,0:T(8,128)S(1)}, u32[]{:S(2)}, u32[]{:S(2)}) collective-permute-start(f32[2,128,2,128]{3,1,2,0:T(8,128)S(1)} %maximum_add_fusion.2), channel_id=1, source_target_pairs={{0,1},{1,2},{2,3},{3,4},{4,5},{5,6},{6,7},{7,8},{8,9},{9,10},{10,1... | collective-permute-start | bytes 786440 | tf_op jit(solution)/shard_map/while/body/eval_jaxpr/ppermute | solution.py:14
  120.2 9.5 %collective-permute-start.1 = (f32[2,128,2,128]{3,1,2,0:T(8,128)S(1)}, f32[2,128,2,128]{3,1,2,0:T(8,128)S(1)}, u32[]{:S(2)}, u32[]{:S(2)}) collective-permute-start(f32[2,128,2,128]{3,1,2,0:T(8,128)S(1)} %maximum_add_fusion.2), channel_id=1, source_target_pairs={{0,1},{1,2},{2,3},{3,4},{4,5},{5,6},{6,7},{7,8},{8,9},{9,10},{10,1... | collective-permute-start | bytes 786440 | tf_op jit(solution)/shard_map/while/body/eval_jaxpr/ppermute | solution.py:14
  131.6 9.5 %collective-permute-start.1 = (f32[2,128,2,128]{3,1,2,0:T(8,128)S(1)}, f32[2,128,2,128]{3,1,2,0:T(8,128)S(1)}, u32[]{:S(2)}, u32[]{:S(2)}) collective-permute-start(f32[2,128,2,128]{3,1,2,0:T(8,128)S(1)} %maximum_add_fusion.2), channel_id=1, source_target_pairs={{0,1},{1,2},{2,3},{3,4},{4,5},{5,6},{6,7},{7,8},{8,9},{9,10},{10,1... | collective-permute-start | bytes 786440 | tf_op jit(solution)/shard_map/while/body/eval_jaxpr/ppermute | solution.py:14
  143.0 9.5 %collective-permute-start.1 = (f32[2,128,2,128]{3,1,2,0:T(8,128)S(1)}, f32[2,128,2,128]{3,1,2,0:T(8,128)S(1)}, u32[]{:S(2)}, u32[]{:S(2)}) collective-permute-start(f32[2,128,2,128]{3,1,2,0:T(8,128)S(1)} %maximum_add_fusion.2), channel_id=1, source_target_pairs={{0,1},{1,2},{2,3},{3,4},{4,5},{5,6},{6,7},{7,8},{8,9},{9,10},{10,1... | collective-permute-start | bytes 786440 | tf_op jit(solution)/shard_map/while/body/eval_jaxpr/ppermute | solution.py:14
  154.4 9.5 %collective-permute-start.1 = (f32[2,128,2,128]{3,1,2,0:T(8,128)S(1)}, f32[2,128,2,128]{3,1,2,0:T(8,128)S(1)}, u32[]{:S(2)}, u32[]{:S(2)}) collective-permute-start(f32[2,128,2,128]{3,1,2,0:T(8,128)S(1)} %maximum_add_fusion.2), channel_id=1, source_target_pairs={{0,1},{1,2},{2,3},{3,4},{4,5},{5,6},{6,7},{7,8},{8,9},{9,10},{10,1... | collective-permute-start | bytes 786440 | tf_op jit(solution)/shard_map/while/body/eval_jaxpr/ppermute | solution.py:14
  165.8 9.5 %collective-permute-start.1 = (f32[2,128,2,128]{3,1,2,0:T(8,128)S(1)}, f32[2,128,2,128]{3,1,2,0:T(8,128)S(1)}, u32[]{:S(2)}, u32[]{:S(2)}) collective-permute-start(f32[2,128,2,128]{3,1,2,0:T(8,128)S(1)} %maximum_add_fusion.2), channel_id=1, source_target_pairs={{0,1},{1,2},{2,3},{3,4},{4,5},{5,6},{6,7},{7,8},{8,9},{9,10},{10,1... | collective-permute-start | bytes 786440 | tf_op jit(solution)/shard_map/while/body/eval_jaxpr/ppermute | solution.py:14
  177.2 9.5 %collective-permute-start.1 = (f32[2,128,2,128]{3,1,2,0:T(8,128)S(1)}, f32[2,128,2,128]{3,1,2,0:T(8,128)S(1)}, u32[]{:S(2)}, u32[]{:S(2)}) collective-permute-start(f32[2,128,2,128]{3,1,2,0:T(8,128)S(1)} %maximum_add_fusion.2), channel_id=1, source_target_pairs={{0,1},{1,2},{2,3},{3,4},{4,5},{5,6},{6,7},{7,8},{8,9},{9,10},{10,1... | collective-permute-start | bytes 786440 | tf_op jit(solution)/shard_map/while/body/eval_jaxpr/ppermute | solution.py:14
  188.6 9.5 %collective-permute-start.1 = (f32[2,128,2,128]{3,1,2,0:T(8,128)S(1)}, f32[2,128,2,128]{3,1,2,0:T(8,128)S(1)}, u32[]{:S(2)}, u32[]{:S(2)}) collective-permute-start(f32[2,128,2,128]{3,1,2,0:T(8,128)S(1)} %maximum_add_fusion.2), channel_id=1, source_target_pairs={{0,1},{1,2},{2,3},{3,4},{4,5},{5,6},{6,7},{7,8},{8,9},{9,10},{10,1... | collective-permute-start | bytes 786440 | tf_op jit(solution)/shard_map/while/body/eval_jaxpr/ppermute | solution.py:14
  200.0 9.5 %collective-permute-start.1 = (f32[2,128,2,128]{3,1,2,0:T(8,128)S(1)}, f32[2,128,2,128]{3,1,2,0:T(8,128)S(1)}, u32[]{:S(2)}, u32[]{:S(2)}) collective-permute-start(f32[2,128,2,128]{3,1,2,0:T(8,128)S(1)} %maximum_add_fusion.2), channel_id=1, source_target_pairs={{0,1},{1,2},{2,3},{3,4},{4,5},{5,6},{6,7},{7,8},{8,9},{9,10},{10,1... | collective-permute-start | bytes 786440 | tf_op jit(solution)/shard_map/while/body/eval_jaxpr/ppermute | solution.py:14
  211.4 9.5 %collective-permute-start.1 = (f32[2,128,2,128]{3,1,2,0:T(8,128)S(1)}, f32[2,128,2,128]{3,1,2,0:T(8,128)S(1)}, u32[]{:S(2)}, u32[]{:S(2)}) collective-permute-start(f32[2,128,2,128]{3,1,2,0:T(8,128)S(1)} %maximum_add_fusion.2), channel_id=1, source_target_pairs={{0,1},{1,2},{2,3},{3,4},{4,5},{5,6},{6,7},{7,8},{8,9},{9,10},{10,1... | collective-permute-start | bytes 786440 | tf_op jit(solution)/shard_map/while/body/eval_jaxpr/ppermute | solution.py:14
  222.8 9.5 %collective-permute-start.1 = (f32[2,128,2,128]{3,1,2,0:T(8,128)S(1)}, f32[2,128,2,128]{3,1,2,0:T(8,128)S(1)}, u32[]{:S(2)}, u32[]{:S(2)}) collective-permute-start(f32[2,128,2,128]{3,1,2,0:T(8,128)S(1)} %maximum_add_fusion.2), channel_id=1, source_target_pairs={{0,1},{1,2},{2,3},{3,4},{4,5},{5,6},{6,7},{7,8},{8,9},{9,10},{10,1... | collective-permute-start | bytes 786440 | tf_op jit(solution)/shard_map/while/body/eval_jaxpr/ppermute | solution.py:14
  234.2 9.5 %collective-permute-start.1 = (f32[2,128,2,128]{3,1,2,0:T(8,128)S(1)}, f32[2,128,2,128]{3,1,2,0:T(8,128)S(1)}, u32[]{:S(2)}, u32[]{:S(2)}) collective-permute-start(f32[2,128,2,128]{3,1,2,0:T(8,128)S(1)} %maximum_add_fusion.2), channel_id=1, source_target_pairs={{0,1},{1,2},{2,3},{3,4},{4,5},{5,6},{6,7},{7,8},{8,9},{9,10},{10,1... | collective-permute-start | bytes 786440 | tf_op jit(solution)/shard_map/while/body/eval_jaxpr/ppermute | solution.py:14
  245.6 9.5 %collective-permute-start.1 = (f32[2,128,2,128]{3,1,2,0:T(8,128)S(1)}, f32[2,128,2,128]{3,1,2,0:T(8,128)S(1)}, u32[]{:S(2)}, u32[]{:S(2)}) collective-permute-start(f32[2,128,2,128]{3,1,2,0:T(8,128)S(1)} %maximum_add_fusion.2), channel_id=1, source_target_pairs={{0,1},{1,2},{2,3},{3,4},{4,5},{5,6},{6,7},{7,8},{8,9},{9,10},{10,1... | collective-permute-start | bytes 786440 | tf_op jit(solution)/shard_map/while/body/eval_jaxpr/ppermute | solution.py:14
  257.0 9.5 %collective-permute-start.1 = (f32[2,128,2,128]{3,1,2,0:T(8,128)S(1)}, f32[2,128,2,128]{3,1,2,0:T(8,128)S(1)}, u32[]{:S(2)}, u32[]{:S(2)}) collective-permute-start(f32[2,128,2,128]{3,1,2,0:T(8,128)S(1)} %maximum_add_fusion.2), channel_id=1, source_target_pairs={{0,1},{1,2},{2,3},{3,4},{4,5},{5,6},{6,7},{7,8},{8,9},{9,10},{10,1... | collective-permute-start | bytes 786440 | tf_op jit(solution)/shard_map/while/body/eval_jaxpr/ppermute | solution.py:14
  268.4 9.5 %collective-permute-start.1 = (f32[2,128,2,128]{3,1,2,0:T(8,128)S(1)}, f32[2,128,2,128]{3,1,2,0:T(8,128)S(1)}, u32[]{:S(2)}, u32[]{:S(2)}) collective-permute-start(f32[2,128,2,128]{3,1,2,0:T(8,128)S(1)} %maximum_add_fusion.2), channel_id=1, source_target_pairs={{0,1},{1,2},{2,3},{3,4},{4,5},{5,6},{6,7},{7,8},{8,9},{9,10},{10,1... | collective-permute-start | bytes 786440 | tf_op jit(solution)/shard_map/while/body/eval_jaxpr/ppermute | solution.py:14
  279.7 9.5 %collective-permute-start.1 = (f32[2,128,2,128]{3,1,2,0:T(8,128)S(1)}, f32[2,128,2,128]{3,1,2,0:T(8,128)S(1)}, u32[]{:S(2)}, u32[]{:S(2)}) collective-permute-start(f32[2,128,2,128]{3,1,2,0:T(8,128)S(1)} %maximum_add_fusion.2), channel_id=1, source_target_pairs={{0,1},{1,2},{2,3},{3,4},{4,5},{5,6},{6,7},{7,8},{8,9},{9,10},{10,1... | collective-permute-start | bytes 786440 | tf_op jit(solution)/shard_map/while/body/eval_jaxpr/ppermute | solution.py:14
  291.1 9.5 %collective-permute-start.1 = (f32[2,128,2,128]{3,1,2,0:T(8,128)S(1)}, f32[2,128,2,128]{3,1,2,0:T(8,128)S(1)}, u32[]{:S(2)}, u32[]{:S(2)}) collective-permute-start(f32[2,128,2,128]{3,1,2,0:T(8,128)S(1)} %maximum_add_fusion.2), channel_id=1, source_target_pairs={{0,1},{1,2},{2,3},{3,4},{4,5},{5,6},{6,7},{7,8},{8,9},{9,10},{10,1... | collective-permute-start | bytes 786440 | tf_op jit(solution)/shard_map/while/body/eval_jaxpr/ppermute | solution.py:14
  302.5 9.5 %collective-permute-start.1 = (f32[2,128,2,128]{3,1,2,0:T(8,128)S(1)}, f32[2,128,2,128]{3,1,2,0:T(8,128)S(1)}, u32[]{:S(2)}, u32[]{:S(2)}) collective-permute-start(f32[2,128,2,128]{3,1,2,0:T(8,128)S(1)} %maximum_add_fusion.2), channel_id=1, source_target_pairs={{0,1},{1,2},{2,3},{3,4},{4,5},{5,6},{6,7},{7,8},{8,9},{9,10},{10,1... | collective-permute-start | bytes 786440 | tf_op jit(solution)/shard_map/while/body/eval_jaxpr/ppermute | solution.py:14
  313.9 9.5 %collective-permute-start.1 = (f32[2,128,2,128]{3,1,2,0:T(8,128)S(1)}, f32[2,128,2,128]{3,1,2,0:T(8,128)S(1)}, u32[]{:S(2)}, u32[]{:S(2)}) collective-permute-start(f32[2,128,2,128]{3,1,2,0:T(8,128)S(1)} %maximum_add_fusion.2), channel_id=1, source_target_pairs={{0,1},{1,2},{2,3},{3,4},{4,5},{5,6},{6,7},{7,8},{8,9},{9,10},{10,1... | collective-permute-start | bytes 786440 | tf_op jit(solution)/shard_map/while/body/eval_jaxpr/ppermute | solution.py:14
  325.3 9.5 %collective-permute-start.1 = (f32[2,128,2,128]{3,1,2,0:T(8,128)S(1)}, f32[2,128,2,128]{3,1,2,0:T(8,128)S(1)}, u32[]{:S(2)}, u32[]{:S(2)}) collective-permute-start(f32[2,128,2,128]{3,1,2,0:T(8,128)S(1)} %maximum_add_fusion.2), channel_id=1, source_target_pairs={{0,1},{1,2},{2,3},{3,4},{4,5},{5,6},{6,7},{7,8},{8,9},{9,10},{10,1... | collective-permute-start | bytes 786440 | tf_op jit(solution)/shard_map/while/body/eval_jaxpr/ppermute | solution.py:14
  (45 other events, 356.4 us)
where the time goes:
time: 378 us; the launch traced here: 371 us
  waiting for transfers between devices  265 us (70%)
  matrix products  58.9 us (16%)
  starting transfers between devices  20.7 us (5%)
  other arithmetic  12.8 us (3%)
  local copies, waits for them, and re-layouts  9.32 us (2%)
    ppermute x64, waiting for transfers between devices, passed_along(): return lax.ppermute(value, axis, pairs)  265 us
    ppermute x64, starting transfers between devices, passed_along(): return lax.ppermute(value, axis, pairs)  20.7 us
    dot_general x32, matrix products, contribute(): jnp.einsum('gqij,jgd->igqd', dscore, key_heads, preferred_element_type=jn...  15.4 us
    dot_general x32, matrix products, contribute(): jnp.einsum('igqd,jgd->gqij', query_heads, key_heads, preferred_element_ty...  13.9 us
    dot_general x32, matrix products, contribute(): jnp.einsum('igqd,jgd->gqij', dout_heads, value_heads, preferred_element_t...  11.3 us
    dot_general x32, matrix products, contribute(): jnp.einsum('gqij,igqd->jgd', dscore, query_heads, preferred_element_type=...  9.15 us
    dot_general x32, matrix products, contribute(): jnp.einsum('gqij,igqd->jgd', probs_low, dout_heads, preferred_element_typ...  9.13 us
  transfers between devices with their start and end apart: 64, of which 63 were waited for; matrix products, arithmetic and copies ran while one was open for 19% of the time, Pallas kernels for 0%

commit v1 on v0

v1 whole, which is shorter than its diff:
```python
import functools

import jax
import jax.numpy as jnp
from jax import lax
from jax.experimental import pallas as pl
from jax.experimental.pallas import tpu as pltpu
from jax.sharding import PartitionSpec as P

HD = 128
HEADS = 16
GROUPS = 2
HALF = 64
ROWS = 128
QUAD = 4
RING = 8
SEQ = ROWS * QUAD * RING
SHARD = ROWS * QUAD
COLS = HEADS * HD // QUAD
MEMBER_HEADS = HEADS // QUAD
TILE = 4
MESH = pl.DeviceIdType.MESH
INV_ROOT = HD ** (-0.5)
LOG2E = 1.4426950408889634
F32 = jnp.float32
BF16 = jnp.bfloat16


def place():
    me = lax.axis_index("ctx")
    return lax.axis_index("dp"), me // QUAD, lax.rem(me, QUAD)


def device(dp, z, member):
    return (dp, lax.rem(z + RING, RING) * QUAD + member)


def greet(dp, z, r):
    barrier = pltpu.get_barrier_semaphore()
    for dz in (1, -1):
        for t in range(QUAD):
            pl.semaphore_signal(barrier, inc=1, device_id=device(dp, z + dz, t), device_id_type=MESH)
    for other in range(1, QUAD):
        pl.semaphore_signal(barrier, inc=1, device_id=device(dp, z, r ^ other), device_id_type=MESH)
    return lambda: pl.semaphore_wait(barrier, 2 * QUAD + QUAD - 1)


def rows_at(start, count):
    return pl.ds(pl.multiple_of(start, count), count)


def remote(src, dst, send_sem, recv_sem, target):
    return pltpu.make_async_remote_copy(
        src_ref=src, dst_ref=dst, send_sem=send_sem, recv_sem=recv_sem, device_id=target, device_id_type=MESH
    )


def split_lanes(table, half):
    pieces = []
    for t in range(QUAD):
        heads = [
            table[t * MEMBER_HEADS + e : t * MEMBER_HEADS + e + 1, half * HALF : (half + 1) * HALF]
            for e in range(MEMBER_HEADS)
        ]
        pieces.append(jnp.concatenate(heads, axis=1))
    return jnp.concatenate(pieces, axis=0)


def gather_kernel(
    q_ref, k_ref, v_ref, o_ref, do_ref, lse_ref,
    qg_ref, dog_ref, kv_ref, ld_ref,
    o_vm, do_vm, ld_vm,
    load_sem, first_send, first_own, own_recv, other_recv, ring_send, core_send, head_send, head_recv, head_own,
):
    dp, z, r = place()
    core = lax.rem(r, 2)
    greeted = greet(dp, z, r)
    loads = [
        pltpu.make_async_copy(o_ref, o_vm, load_sem.at[0]),
        pltpu.make_async_copy(do_ref, do_vm, load_sem.at[1]),
    ]
    for c in loads:
        c.start()
    greeted()

    def kv_rows(shard, member):
        return rows_at((lax.rem(shard + RING, RING) * QUAD + member) * ROWS, ROWS)

    first = []
    mine = kv_rows(z, r)
    for i, dz in enumerate((1, -1, 0)):
        for t in range(QUAD):
            source = (v_ref if t % 2 else k_ref).at[:, (t // 2) * HD : (t // 2 + 1) * HD]
            target = kv_ref.at[t % 2, mine, :]
            copy = remote(source, target, first_send.at[i, t], own_recv.at[dz % RING, r], device(dp, z + dz, t))
            if dz:
                copy.start()
                first.append(copy)
            else:
                @pl.when(t != r)
                def _():
                    copy.start()

                @pl.when(t == r)
                def _():
                    pltpu.make_async_copy(source, target, first_own).start()

    heads = []
    for i, (src, dst) in enumerate(((q_ref, qg_ref), (do_ref, dog_ref))):
        to_rows = rows_at(r * ROWS, ROWS)
        for other in range(1, QUAD):
            t = r ^ other
            cols = rows_at(t * COLS, COLS)
            copy = remote(
                src.at[:, cols], dst.at[to_rows, :], head_send.at[i, other], head_recv.at[i, other], device(dp, z, t)
            )
            copy.start()
            heads.append(copy)
        own = pltpu.make_async_copy(src.at[:, rows_at(r * COLS, COLS)], dst.at[to_rows, :], head_own.at[i])
        own.start()
        heads.append(own)

    for c in loads:
        c.wait()
    prod = do_vm[...].astype(F32) * o_vm[...].astype(F32)
    high = prod.astype(BF16)
    low = (prod - high.astype(F32)).astype(BF16)
    head_of = lax.broadcasted_iota(jnp.int32, (HEADS, HEADS * HD), 1) // HD
    ones = (head_of == lax.broadcasted_iota(jnp.int32, (HEADS, HEADS * HD), 0)).astype(BF16)
    along = (((1,), (1,)), ((), ()))
    delta = lax.dot_general(ones, high, along, preferred_element_type=F32) + lax.dot_general(
        ones, low, along, preferred_element_type=F32
    )
    for half in range(2):
        ld_vm[0, half] = split_lanes(lse_ref[...] * LOG2E, half)
        ld_vm[1, half] = split_lanes(delta, half)
    for other in range(1, QUAD):
        copy = remote(ld_vm, ld_ref.at[r], head_send.at[2, other], head_recv.at[2, other], device(dp, z, r ^ other))
        copy.start()
        heads.append(copy)
    own = pltpu.make_async_copy(ld_vm, ld_ref.at[r], head_own.at[2])
    own.start()
    heads.append(own)

    forwards = []
    crossings = []

    def slot(k, p):
        return kv_ref.at[core, kv_rows(z - k, p), :]

    def arrived(k, p):
        piece = slot(k, p)
        remote(piece, piece, first_send.at[0, 0], own_recv.at[k, p], device(dp, z, r ^ 1)).wait_recv()
        return piece

    def forward(k, p, step, piece):
        i = 0 if step > 0 else 1
        copy = remote(piece, piece, ring_send.at[i, k, p], own_recv.at[k + step, p], device(dp, z + step, r))
        copy.start()
        forwards.append(copy)

    def cross(k, p, piece):
        copy = remote(piece, piece, core_send.at[k, p], other_recv.at[k, p], device(dp, z, r ^ 1))
        copy.start()
        crossings.append((copy, k, p))

    for k in range(1, 4):
        for p in range(QUAD):
            piece = arrived(k, p)
            if k < 3 or p < 2:
                forward(k, p, 1, piece)
            cross(k, p, piece)
            piece = arrived(RING - k, p)
            if k < 3 or p >= 2:
                forward(RING - k, p, -1, piece)
            cross(RING - k, p, piece)
        if k == 1:
            for p in range(QUAD):
                piece = slot(0, p)

                @pl.when(p != r)
                def _():
                    arrived(0, p)

                @pl.when(p == r)
                def _():
                    pltpu.make_async_copy(piece, piece, first_own).wait()

                cross(0, p, piece)
    for p in range(QUAD):
        cross(4, p, arrived(4, p))
    for copy, k, p in crossings:
        copy.wait_send()
        theirs = kv_ref.at[1 - core, kv_rows(z - k, p), :]
        remote(theirs, theirs, core_send.at[k, p], other_recv.at[k, p], device(dp, z, r ^ 1)).wait_recv()
    for copy in forwards + first:
        copy.wait_send()
    for t in range(QUAD):
        @pl.when(t != r)
        def _():
            piece = slot(0, 0)
            remote(piece, piece, first_send.at[2, t], own_recv.at[0, 0], device(dp, z, r ^ 1)).wait_send()
    for copy in heads:
        copy.wait()


def dot_tt(a, b):
    return lax.dot_general(a, b, (((1,), (1,)), ((), ())), preferred_element_type=F32)


def attend_kernel(doc_ref, order_ref, q_ref, do_ref, kv_ref, ld_ref, dq_ref, dkv_ref, acc_ref, dqt_ref, inv_ref):
    _, z, r = place()
    lanes = MEMBER_HEADS * HALF

    @pl.loop(0, SEQ // HALF)
    def _(s):
        inv_ref[order_ref[s]] = s

    acc_ref[...] = jnp.zeros_like(acc_ref)

    def query_block(member, half):
        b = order_ref[(z * QUAD + member) * 2 + half]
        low = b * HALF
        tok_q = low + lax.broadcasted_iota(jnp.int32, (1, lanes), 1) % HALF
        begin_q = jnp.zeros((1, lanes), jnp.int32)
        begin = jnp.int32(0)
        end = jnp.int32(0)
        for d in range(doc_ref.shape[0]):
            end = end + doc_ref[d]
            begin = jnp.where(end <= low, end, begin)
            begin_q = jnp.where(end <= tok_q, end, begin_q)
        tiles = (b - begin // HALF) // TILE + 1
        rows = rows_at((member * 2 + half) * HALF, HALF)
        q = jnp.concatenate([q_ref[rows, e * HD : (e + 1) * HD] for e in range(MEMBER_HEADS)], axis=0)
        do = jnp.concatenate([do_ref[rows, e * HD : (e + 1) * HD] for e in range(MEMBER_HEADS)], axis=0)
        lse = ld_ref[member, 0, half, pl.ds(r, 1), :]
        delta = ld_ref[member, 1, half, pl.ds(r, 1), :]
        dqt_ref[...] = jnp.zeros_like(dqt_ref)

        @pl.loop(0, tiles)
        def _(t):
            base = b - TILE * t - (TILE - 1)
            spans = [rows_at(inv_ref[jnp.maximum(base + j, 0)] * HALF, HALF) for j in range(TILE)]
            k = jnp.concatenate([kv_ref[0, span, :] for span in spans], axis=0)
            v = jnp.concatenate([kv_ref[1, span, :] for span in spans], axis=0)
            tok_k = base * HALF + lax.broadcasted_iota(jnp.int32, (TILE * HALF, 1), 0)
            visible = (tok_k <= tok_q) & (tok_k >= begin_q)
            score = dot_tt(k, q)
            probs = jnp.exp2(jnp.where(visible, score * (INV_ROOT * LOG2E) - lse, -1e30))
            dprobs = dot_tt(v, do)
            dscore = (probs * (dprobs - delta)).astype(BF16)
            probs_low = probs.astype(BF16)
            dv = jnp.dot(probs_low, do, preferred_element_type=F32)
            dk = jnp.dot(dscore, q, preferred_element_type=F32)
            dqt_ref[...] += lax.dot_general(k, dscore, (((0,), (0,)), ((), ())), preferred_element_type=F32)
            for j, span in enumerate(spans):
                acc_ref[0, span, :] += dk[j * HALF : (j + 1) * HALF]
                acc_ref[1, span, :] += dv[j * HALF : (j + 1) * HALF]

        dq = (dqt_ref[...].T * INV_ROOT).astype(BF16)
        for e in range(MEMBER_HEADS):
            dq_ref[rows, e * HD : (e + 1) * HD] = dq[e * HALF : (e + 1) * HALF]

    @pl.loop(0, QUAD)
    def _(member):
        for half in range(2):
            query_block(member, half)

    @pl.loop(0, SEQ // SHARD)
    def _(i):
        span = rows_at(i * SHARD, SHARD)
        dkv_ref[0, span, :] = (acc_ref[0, span, :] * INV_ROOT).astype(BF16)
        dkv_ref[1, span, :] = acc_ref[1, span, :].astype(BF16)


def reduce_kernel(
    dq_ref, dkv_ref,
    qgrad_ref, kgrad_ref, vgrad_ref,
    own_vm, other_vm, recv_vm, send_vm, last_vm, final_vm,
    load_sem, core_send, core_recv, ring_send, ring_recv, last_send, last_recv, head_send, head_recv, head_own,
):
    dp, z, r = place()
    core = lax.rem(r, 2)
    greeted = greet(dp, z, r)

    def shard(d):
        return rows_at(lax.rem(z + d + RING, RING) * SHARD, SHARD)

    def piece(d, p):
        return rows_at((lax.rem(z + d + RING, RING) * QUAD + p) * ROWS, ROWS)

    order = (4, 3, 5, 2, 6, 1, 7, 0)
    loads = {}
    for d in order:
        loads[d] = pltpu.make_async_copy(dkv_ref.at[core, shard(d), :], own_vm.at[shard(d), :], load_sem.at[d])
        loads[d].start()
    greeted()
    crossings = {}
    for d in order:
        crossings[d] = remote(
            dkv_ref.at[1 - core, shard(d), :], other_vm.at[shard(d), :], core_send.at[d], core_recv.at[d],
            device(dp, z, r ^ 1),
        )
        crossings[d].start()
    heads = []
    to_cols = rows_at(r * COLS, COLS)
    for other in range(1, QUAD):
        t = r ^ other
        copy = remote(
            dq_ref.at[rows_at(t * ROWS, ROWS), :], qgrad_ref.at[:, to_cols],
            head_send.at[other], head_recv.at[other], device(dp, z, t),
        )
        copy.start()
        heads.append(copy)
    own = pltpu.make_async_copy(dq_ref.at[rows_at(r * ROWS, ROWS), :], qgrad_ref.at[:, to_cols], head_own)
    own.start()
    heads.append(own)

    def total(d, p):
        return own_vm[piece(d, p), :].astype(F32) + other_vm[piece(d, p), :].astype(F32)

    def ready(d):
        loads[d].wait()
        crossings[d].wait_recv()

    sends = []

    def pass_on(i, s, p, value):
        here = send_vm.at[i, s, p]
        here[...] = value.astype(BF16)
        copy = remote(
            here, recv_vm.at[i, s, p], ring_send.at[i, s, p], ring_recv.at[i, s, p],
            device(dp, z + (1 - 2 * i), r),
        )
        copy.start()
        sends.append(copy)

    def came(i, s, p):
        here = recv_vm.at[i, s, p]
        remote(here, here, ring_send.at[i, s, p], ring_recv.at[i, s, p], device(dp, z, r ^ 1)).wait_recv()
        return here[...].astype(F32)

    first_half, second_half = (0, 1), (2, 3)
    ready(4)
    for a, b in zip(first_half, second_half):
        pass_on(0, 0, a, total(4, a))
        pass_on(1, 0, b, total(4, b))
    ready(3)
    ready(5)
    for a, b in zip(second_half, first_half):
        pass_on(0, 1, a, total(3, a))
        pass_on(1, 1, b, total(5, b))
    for a, b in zip(first_half, second_half):
        pass_on(0, 1, a, total(3, a) + came(0, 0, a))
        pass_on(1, 1, b, total(5, b) + came(1, 0, b))
    ready(2)
    ready(6)
    for a, b in zip(second_half + first_half, first_half + second_half):
        pass_on(0, 2, a, total(2, a) + came(0, 1, a))
        pass_on(1, 2, b, total(6, b) + came(1, 1, b))
    ready(1)
    ready(7)
    ready(0)

    def finish(i, d, p, value):
        here = last_vm.at[i, p]
        here[...] = value.astype(BF16)
        there = final_vm.at[i, r]
        copy = remote(here, there, last_send.at[i, p], last_recv.at[i, r], device(dp, z + d, p))
        if d:
            copy.start()
            sends.append(copy)
        else:
            @pl.when(p != r)
            def _():
                copy.start()

            @pl.when(p == r)
            def _():
                there[...] = here[...]

    for p in range(QUAD):
        finish(2, 0, p, total(0, p))
    for a, b in zip(second_half + first_half, first_half + second_half):
        finish(0, 1, a, total(1, a) + came(0, 2, a))
        finish(1, -1, b, total(7, b) + came(1, 2, b))
    for t in range(QUAD):
        for i in range(3):
            here = final_vm.at[i, t]
            arrival = remote(here, here, last_send.at[i, t], last_recv.at[i, t], device(dp, z, r ^ 1))
            if i < 2:
                arrival.wait_recv()
            else:
                @pl.when(t != r)
                def _():
                    arrival.wait_recv()
        value = final_vm[0, t].astype(F32) + final_vm[1, t].astype(F32) + final_vm[2, t].astype(F32)
        out = vgrad_ref if t % 2 else kgrad_ref
        out[:, (t // 2) * HD : (t // 2 + 1) * HD] = value.astype(BF16)
    for p in range(QUAD):
        @pl.when(p != r)
        def _():
            here = last_vm.at[2, p]
            remote(here, here, last_send.at[2, p], last_recv.at[2, p], device(dp, z, r ^ 1)).wait_send()
    for copy in sends:
        copy.wait_send()
    for d in order:
        crossings[d].wait_send()
    for copy in heads:
        copy.wait()


ANY = pl.BlockSpec(memory_space=pl.ANY)
VMEM = pl.BlockSpec(memory_space=pltpu.VMEM)
SMEM = pl.BlockSpec(memory_space=pltpu.SMEM)
DMA = pltpu.SemaphoreType.DMA


def gather(query, keys, values, attn_out, grad_out, log_total):
    return pl.pallas_call(
        gather_kernel,
        out_shape=(
            jax.ShapeDtypeStruct((SHARD, COLS), BF16),
            jax.ShapeDtypeStruct((SHARD, COLS), BF16),
            jax.ShapeDtypeStruct((2, SEQ, HD), BF16),
            jax.ShapeDtypeStruct((QUAD, 2, 2, QUAD, MEMBER_HEADS * HALF), F32),
        ),
        in_specs=[ANY] * 5 + [VMEM],
        out_specs=(ANY, ANY, ANY, ANY),
        scratch_shapes=[
            pltpu.VMEM((ROWS, HEADS * HD), BF16),
            pltpu.VMEM((ROWS, HEADS * HD), BF16),
            pltpu.VMEM((2, 2, QUAD, MEMBER_HEADS * HALF), F32),
            DMA((2,)),
            DMA((3, QUAD)),
            DMA,
            DMA((RING, QUAD)),
            DMA((RING, QUAD)),
            DMA((2, RING, QUAD)),
            DMA((RING, QUAD)),
            DMA((3, QUAD)),
            DMA((3, QUAD)),
            DMA((3,)),
        ],
        compiler_params=pltpu.CompilerParams(
            collective_id=0, has_side_effects=True, vmem_limit_bytes=24 * 2**20
        ),
    )(query, keys, values, attn_out, grad_out, log_total)


def attend(doc_lengths, block_order, q, do, kv, ld):
    return pl.pallas_call(
        attend_kernel,
        out_shape=(
            jax.ShapeDtypeStruct((SHARD, COLS), BF16),
            jax.ShapeDtypeStruct((2, SEQ, HD), BF16),
        ),
        in_specs=[SMEM, SMEM, VMEM, VMEM, VMEM, VMEM],
        out_specs=(VMEM, VMEM),
        scratch_shapes=[
            pltpu.VMEM((2, SEQ, HD), F32),
            pltpu.VMEM((HD, MEMBER_HEADS * HALF), F32),
            pltpu.SMEM((SEQ // HALF,), jnp.int32),
        ],
        compiler_params=pltpu.CompilerParams(vmem_limit_bytes=40 * 2**20),
    )(doc_lengths, block_order, q, do, kv, ld)


def reduce(dq, dkv):
    return pl.pallas_call(
        reduce_kernel,
        out_shape=(
            jax.ShapeDtypeStruct((ROWS, HEADS * HD), BF16),
            jax.ShapeDtypeStruct((ROWS, GROUPS * HD), BF16),
            jax.ShapeDtypeStruct((ROWS, GROUPS * HD), BF16),
        ),
        in_specs=[ANY, ANY],
        out_specs=(ANY, VMEM, VMEM),
        scratch_shapes=[
            pltpu.VMEM((SEQ, HD), BF16),
            pltpu.VMEM((SEQ, HD), BF16),
            pltpu.VMEM((2, 3, QUAD, ROWS, HD), BF16),
            pltpu.VMEM((2, 3, QUAD, ROWS, HD), BF16),
            pltpu.VMEM((3, QUAD, ROWS, HD), BF16),
            pltpu.VMEM((3, QUAD, ROWS, HD), BF16),
            DMA((RING,)),
            DMA((RING,)),
            DMA((RING,)),
            DMA((2, 3, QUAD)),
            DMA((2, 3, QUAD)),
            DMA((3, QUAD)),
            DMA((3, QUAD)),
            DMA((QUAD,)),
            DMA((QUAD,)),
            DMA,
        ],
        compiler_params=pltpu.CompilerParams(
            collective_id=1, has_side_effects=True, vmem_limit_bytes=24 * 2**20
        ),
    )(dq, dkv)


def local(query, keys, values, attn_out, grad_out, log_total, doc_lengths, block_order):
    q, do, kv, ld = gather(query, keys, values, attn_out, grad_out, log_total)
    dq, dkv = attend(doc_lengths, block_order, q, do, kv, ld)
    return reduce(dq, dkv)


def solution(mesh):
    rows = P(("dp", "ctx"), None)
    return jax.shard_map(
        local,
        mesh=mesh,
        in_specs=(rows, rows, rows, rows, rows, P(None, ("dp", "ctx")), P("dp"), P("dp")),
        out_specs=(rows, rows, rows),
        check_vma=False,
    )
```

time: 378 us -> 69 us (0.18); the launches traced: 371 us -> 68 us
  waiting for transfers between devices: 265 us -> 0 us
  matrix products: 58.9 us -> 0 us
  Pallas kernels: 0 us -> 58.5 us
  starting transfers between devices: 20.7 us -> 0 us
  other arithmetic: 12.8 us -> 0 us
    ppermute x64 -> x0, waiting for transfers between devices: 265 us -> none  [passed_along(): return lax.ppermute(value, axis, pairs)]
    dot_general x160 -> x0, matrix products: 58.9 us -> none  [the longest x32 15.4 us: contribute(): jnp.einsum('gqij,jgd->igqd', dscore, key_heads, preferred_element_type=jn...]
    pallas_call x0 -> x3, Pallas kernels: none -> 58.5 us  [the longest x1 27.4 us: gather(): pl.pallas_call(gather_kernel, out_shape=(jax.ShapeDtypeStruct((SHARD, COL...]
    ppermute x64 -> x0, starting transfers between devices: 20.7 us -> none  [passed_along(): return lax.ppermute(value, axis, pairs)]
    reduce_sum x66 -> x0, other arithmetic: 6.72 us -> none  [the longest x33 3.78 us: token_numbers(): jnp.sum(onehot * block_order[None, :], axis=1) * half_rows]
  transfers between devices with their start and end apart: 64 -> 0, of which waited for: 63 -> 0; matrix products, arithmetic and copies ran while one was open for 19% -> 0% of each run, Pallas kernels for 0% -> 0%
where the time goes in v1:
time: 69 us; the launch traced here: 68 us
  Pallas kernels  58.5 us (85%)
  local copies, waits for them, and re-layouts  8.85 us (13%)
    pallas_call x1, Pallas kernels, gather(): pl.pallas_call(gather_kernel, out_shape=(jax.ShapeDtypeStruct((SHARD, COL...  27.4 us
    pallas_call x1, Pallas kernels, reduce(): pl.pallas_call(reduce_kernel, out_shape=(jax.ShapeDtypeStruct((ROWS, HEAD...  22.2 us
    unnamed x19, local copies, waits for them, and re-layouts  8.85 us
    pallas_call x1, Pallas kernels, attend(): pl.pallas_call(attend_kernel, out_shape=(jax.ShapeDtypeStruct((SHARD, COL...  8.85 us

profile of v1, /device:TPU:1, one launch (start us, length us, event | category | flops | bytes accessed | tf_op | source)
XLA Modules:
  0.0 68.0 jit_solution(2671731039762176194)
XLA Ops:
  0.6 0.0 copy-start
  0.6 1.0 %copy-done = bf16[128,2048]{1,0:T(8,128)(2,1)S(1)} copy-done((bf16[128,2048]{1,0:T(8,128)(2,1)S(1)}, bf16[128,2048]{1,0:T(8,128)(2,1)}, u32[]{:S(2)}) %copy-start) | copy-done | bytes 524312
  1.7 0.0 copy-start.1
  1.7 1.0 %copy-done.1 = bf16[128,2048]{1,0:T(8,128)(2,1)S(1)} copy-done((bf16[128,2048]{1,0:T(8,128)(2,1)S(1)}, bf16[128,2048]{1,0:T(8,128)(2,1)}, u32[]{:S(2)}) %copy-start.1) | copy-done | bytes 524312
  2.7 0.0 copy-start.2
  2.7 1.0 %copy-done.2 = bf16[128,2048]{1,0:T(8,128)(2,1)S(1)} copy-done((bf16[128,2048]{1,0:T(8,128)(2,1)S(1)}, bf16[128,2048]{1,0:T(8,128)(2,1)}, u32[]{:S(2)}) %copy-start.2) | copy-done | bytes 524312
  3.8 0.0 copy-start.3
  3.8 0.8 %copy-done.3 = bf16[128,256]{1,0:T(8,128)(2,1)S(1)} copy-done((bf16[128,256]{1,0:T(8,128)(2,1)S(1)}, bf16[128,256]{1,0:T(8,128)(2,1)}, u32[]{:S(2)}) %copy-start.3) | copy-done | bytes 65560
  4.6 0.0 copy-start.4
  4.6 0.8 %copy-done.4 = bf16[128,256]{1,0:T(8,128)(2,1)S(1)} copy-done((bf16[128,256]{1,0:T(8,128)(2,1)S(1)}, bf16[128,256]{1,0:T(8,128)(2,1)}, u32[]{:S(2)}) %copy-start.4) | copy-done | bytes 65560
  5.4 0.0 copy-start.5
  5.4 0.7 %copy-done.5 = f32[16,128]{1,0:T(8,128)S(1)} copy-done((f32[16,128]{1,0:T(8,128)S(1)}, f32[16,128]{1,0:T(8,128)}, u32[]{:S(2)}) %copy-start.5) | copy-done | bytes 8216
  6.1 27.4 %shard_map.103 = (bf16[512,512]{1,0:T(8,128)(2,1)S(1)}, bf16[512,512]{1,0:T(8,128)(2,1)S(1)}, bf16[2,4096,128]{2,1,0:T(8,128)(2,1)S(1)}, f32[4,2,2,4,256]{4,3,2,1,0:T(4,128)S(1)}) custom-call(bf16[128,2048]{1,0:T(8,128)(2,1)S(1)} %copy-done, bf16[128,256]{1,0:T(8,128)(2,1)S(1)} %copy-done.3, bf16[128,256]{1,0:T(8,128)(2,1)S(1)} %copy-done.4, ...), custom_call_target="tpu_custom_call" | custom-call | tf_op jit(solution)/shard_map/pallas_call | solution.py:420
  33.6 0.0 copy-start.6
  33.6 0.6 copy-done.6
  34.2 0.0 copy-start.7
  34.2 0.7 copy-done.7
  34.9 8.8 %shard_map.104 = (bf16[512,512]{1,0:T(8,128)(2,1)S(1)}, bf16[2,4096,128]{2,1,0:T(8,128)(2,1)S(1)}) custom-call(s32[16]{0:T(128)S(1)} %copy-done.6, s32[64]{0:T(128)S(1)} %copy-done.7, bf16[512,512]{1,0:T(8,128)(2,1)S(1)} %get-tuple-element.9.q_ref, bf16[512,512]{1,0:T(8,128)(2,1)S(1)} %get-tuple-element.10.do_ref, ...), custom_call_target="tpu_custom_call" | custom-call | tf_op jit(solution)/shard_map/pallas_call | solution.py:452
  43.7 22.2 %shard_map.105 = (bf16[128,2048]{1,0:T(8,128)(2,1)S(1)}, bf16[128,256]{1,0:T(8,128)(2,1)S(1)}, bf16[128,256]{1,0:T(8,128)(2,1)S(1)}) custom-call(bf16[512,512]{1,0:T(8,128)(2,1)S(1)} %get-tuple-element.13.dq_ref, bf16[2,4096,128]{2,1,0:T(8,128)(2,1)S(1)} %get-tuple-element.14.dkv_ref), custom_call_target="tpu_custom_call" | custom-call | tf_op jit(solution)/shard_map/pallas_call | solution.py:470
  65.9 0.8 %copy.14 = bf16[128,2048]{1,0:T(8,128)(2,1)} copy(bf16[128,2048]{1,0:T(8,128)(2,1)S(1)} %get-tuple-element.18) | data formatting | bytes 1048576
  66.7 0.6 copy.15
  67.4 0.6 copy.16
Async XLA Ops:
  0.6 1.0 %copy-start = (bf16[128,2048]{1,0:T(8,128)(2,1)S(1)}, bf16[128,2048]{1,0:T(8,128)(2,1)}, u32[]{:S(2)}) copy-start(bf16[128,2048]{1,0:T(8,128)(2,1)} %q_ref.1) | copy-start | bytes 1572868
  1.7 1.0 %copy-start.1 = (bf16[128,2048]{1,0:T(8,128)(2,1)S(1)}, bf16[128,2048]{1,0:T(8,128)(2,1)}, u32[]{:S(2)}) copy-start(bf16[128,2048]{1,0:T(8,128)(2,1)} %o_ref.1) | copy-start | bytes 1572868
  2.7 1.0 %copy-start.2 = (bf16[128,2048]{1,0:T(8,128)(2,1)S(1)}, bf16[128,2048]{1,0:T(8,128)(2,1)}, u32[]{:S(2)}) copy-start(bf16[128,2048]{1,0:T(8,128)(2,1)} %do_ref.1) | copy-start | bytes 1572868
  3.8 0.8 %copy-start.3 = (bf16[128,256]{1,0:T(8,128)(2,1)S(1)}, bf16[128,256]{1,0:T(8,128)(2,1)}, u32[]{:S(2)}) copy-start(bf16[128,256]{1,0:T(8,128)(2,1)} %k_ref.1) | copy-start | bytes 196612
  4.6 0.8 %copy-start.4 = (bf16[128,256]{1,0:T(8,128)(2,1)S(1)}, bf16[128,256]{1,0:T(8,128)(2,1)}, u32[]{:S(2)}) copy-start(bf16[128,256]{1,0:T(8,128)(2,1)} %v_ref.1) | copy-start | bytes 196612
  5.4 0.7 %copy-start.5 = (f32[16,128]{1,0:T(8,128)S(1)}, f32[16,128]{1,0:T(8,128)}, u32[]{:S(2)}) copy-start(f32[16,128]{1,0:T(8,128)} %lse_ref.1) | copy-start | bytes 24580
  33.6 0.7 copy-start.6
  34.2 0.7 copy-start.7

commit v2 on v1

v2 whole, which is shorter than its diff:
```python
import functools

import jax
import jax.numpy as jnp
from jax import lax
from jax.experimental import pallas as pl
from jax.experimental.pallas import tpu as pltpu
from jax.sharding import PartitionSpec as P

HD = 128
HEADS = 16
GROUPS = 2
HALF = 64
ROWS = 128
QUAD = 4
RING = 8
SEQ = ROWS * QUAD * RING
SHARD = ROWS * QUAD
COLS = HEADS * HD // QUAD
MEMBER_HEADS = HEADS // QUAD
WINDOW = 1024 // HALF + 1
TILES = ((0, WINDOW),)
NDOC = 16
BLOCKS = SEQ // HALF
BLOCKS_HERE = SHARD // HALF
LANES = MEMBER_HEADS * HALF
MESH = pl.DeviceIdType.MESH
INV_ROOT = HD ** (-0.5)
LOG2E = 1.4426950408889634
F32 = jnp.float32
BF16 = jnp.bfloat16


def place():
    me = lax.axis_index("ctx")
    return lax.axis_index("dp"), me // QUAD, lax.rem(me, QUAD)


def device(dp, z, member):
    return (dp, lax.rem(z + RING, RING) * QUAD + member)


def greet(dp, z, r):
    barrier = pltpu.get_barrier_semaphore()
    for dz in (1, -1):
        for t in range(QUAD):
            pl.semaphore_signal(barrier, inc=1, device_id=device(dp, z + dz, t), device_id_type=MESH)
    for other in range(1, QUAD):
        pl.semaphore_signal(barrier, inc=1, device_id=device(dp, z, r ^ other), device_id_type=MESH)
    return lambda: pl.semaphore_wait(barrier, 2 * QUAD + QUAD - 1)


def rows_at(start, count):
    return pl.ds(pl.multiple_of(start, count), count)


def remote(src, dst, send_sem, recv_sem, target):
    return pltpu.make_async_remote_copy(
        src_ref=src, dst_ref=dst, send_sem=send_sem, recv_sem=recv_sem, device_id=target, device_id_type=MESH
    )


def split_lanes(table, half):
    pieces = []
    for t in range(QUAD):
        heads = [
            table[t * MEMBER_HEADS + e : t * MEMBER_HEADS + e + 1, half * HALF : (half + 1) * HALF]
            for e in range(MEMBER_HEADS)
        ]
        pieces.append(jnp.concatenate(heads, axis=1))
    return jnp.concatenate(pieces, axis=0)


def dot_tt(a, b):
    return lax.dot_general(a, b, (((1,), (1,)), ((), ())), preferred_element_type=F32)


def attend(z, r, qg_ref, dog_ref, kv_ref, ld_ref, order_sm, slot_sm, begin_vm, part_vm, dq_ref):
    @pl.loop(0, BLOCKS_HERE)
    def _(block):
        b = order_sm[z * BLOCKS_HERE + block]
        tok_q = b * HALF + lax.broadcasted_iota(jnp.int32, (1, LANES), 1) % HALF
        begin_q = begin_vm[block]
        rows = rows_at(block * HALF, HALF)
        q = jnp.concatenate([qg_ref[rows, e * HD : (e + 1) * HD] for e in range(MEMBER_HEADS)], axis=0)
        do = jnp.concatenate([dog_ref[rows, e * HD : (e + 1) * HD] for e in range(MEMBER_HEADS)], axis=0)
        lse = ld_ref[block // 2, 0, lax.rem(block, 2), pl.ds(r, 1), :]
        delta = ld_ref[block // 2, 1, lax.rem(block, 2), pl.ds(r, 1), :]
        dqt = jnp.zeros((HD, LANES), F32)
        for first, last in TILES:
            base = b - (WINDOW - 1) + first
            places = [slot_sm[block, j] for j in range(first, last)]
            k = jnp.concatenate([kv_ref[0, place] for place in places], axis=0)
            v = jnp.concatenate([kv_ref[1, place] for place in places], axis=0)
            tok_k = base * HALF + lax.broadcasted_iota(jnp.int32, ((last - first) * HALF, 1), 0)
            visible = (tok_k <= tok_q) & (tok_k >= begin_q)
            score = dot_tt(k, q)
            probs = jnp.exp2(jnp.where(visible, score * (INV_ROOT * LOG2E) - lse, -1e30))
            dprobs = dot_tt(v, do)
            dscore = (probs * (dprobs - delta)).astype(BF16)
            probs_low = probs.astype(BF16)
            there = slice(first + 1, last + 1)
            blocks = (last - first, HALF, HD)
            part_vm[1, block, there] = jnp.dot(probs_low, do, preferred_element_type=F32).reshape(blocks)
            part_vm[0, block, there] = jnp.dot(dscore, q, preferred_element_type=F32).reshape(blocks)
            dqt += lax.dot_general(k, dscore, (((0,), (0,)), ((), ())), preferred_element_type=F32)
        dq = (dqt.T * INV_ROOT).astype(BF16)
        for e in range(MEMBER_HEADS):
            dq_ref[rows, e * HD : (e + 1) * HD] = dq[e * HALF : (e + 1) * HALF]


def kernel(
    q_ref, k_ref, v_ref, o_ref, do_ref, lse_ref, doc_ref, order_ref,
    qgrad_ref, kgrad_ref, vgrad_ref,
    o_vm, do_vm, own_kv, lse_vm, ld_vm, qg_ref, dog_ref, kv_ref, ld_ref,
    doc_sm, order_sm, slot_vm, slot_sm, begin_vm, part_vm, dq_ref,
    own_vm, give_vm, other_vm, recv_vm, send_vm, last_vm, final_vm,
    load_sem, own_sem, first_send, first_own, own_recv, other_recv, ring_send, core_send, head_send, head_recv, head_own,
    give_send, give_recv, sum_send, sum_recv, last_send, last_recv, back_send, back_recv, back_own,
):
    dp, z, r = place()
    core = lax.rem(r, 2)
    greeted = greet(dp, z, r)
    loads = [
        pltpu.make_async_copy(o_ref, o_vm, load_sem.at[0]),
        pltpu.make_async_copy(do_ref, do_vm, load_sem.at[1]),
        pltpu.make_async_copy(lse_ref, lse_vm, load_sem.at[2]),
        pltpu.make_async_copy(doc_ref, doc_sm, load_sem.at[3]),
        pltpu.make_async_copy(order_ref, order_sm, load_sem.at[4]),
    ]
    own = []
    for i, (source, kind, g, half) in enumerate(
        (ref, kind, g, half) for kind, ref in ((0, k_ref), (1, v_ref)) for g in range(GROUPS) for half in range(2)
    ):
        block = source.at[half * HALF : (half + 1) * HALF, g * HD : (g + 1) * HD]
        own.append(pltpu.make_async_copy(block, own_kv.at[kind, g, half], own_sem.at[i]))
    for c in own + loads:
        c.start()
    for c in loads[:3]:
        c.wait()
    prod = do_vm[...].astype(F32) * o_vm[...].astype(F32)
    high = prod.astype(BF16)
    low = (prod - high.astype(F32)).astype(BF16)
    head_of = lax.broadcasted_iota(jnp.int32, (HEADS, HEADS * HD), 1) // HD
    ones = (head_of == lax.broadcasted_iota(jnp.int32, (HEADS, HEADS * HD), 0)).astype(BF16)
    along = (((1,), (1,)), ((), ()))
    delta = lax.dot_general(ones, high, along, preferred_element_type=F32) + lax.dot_general(
        ones, low, along, preferred_element_type=F32
    )
    for half in range(2):
        ld_vm[0, half] = split_lanes(lse_vm[...] * LOG2E, half)
        ld_vm[1, half] = split_lanes(delta, half)
    for c in own:
        c.wait()
    greeted()

    def kv_rows(shard, member):
        return pl.ds((lax.rem(shard + RING, RING) * QUAD + member) * 2, 2)

    first = []
    mine = kv_rows(z, r)
    for i, dz in enumerate((1, -1, 0)):
        for t in range(QUAD):
            source = own_kv.at[t % 2, t // 2]
            target = kv_ref.at[t % 2, mine]
            copy = remote(source, target, first_send.at[i, t], own_recv.at[dz % RING, r], device(dp, z + dz, t))
            if dz:
                copy.start()
                first.append(copy)
            else:
                @pl.when(t != r)
                def _():
                    copy.start()

                @pl.when(t == r)
                def _():
                    pltpu.make_async_copy(source, target, first_own).start()

    heads = []
    for i, (src, dst) in enumerate(((q_ref, qg_ref), (do_ref, dog_ref))):
        to_rows = rows_at(r * ROWS, ROWS)
        for other in range(1, QUAD):
            t = r ^ other
            cols = rows_at(t * COLS, COLS)
            copy = remote(
                src.at[:, cols], dst.at[to_rows, :], head_send.at[i, other], head_recv.at[i, other], device(dp, z, t)
            )
            copy.start()
            heads.append(copy)
        own = pltpu.make_async_copy(src.at[:, rows_at(r * COLS, COLS)], dst.at[to_rows, :], head_own.at[i])
        own.start()
        heads.append(own)

    for other in range(1, QUAD):
        copy = remote(ld_vm, ld_ref.at[r], head_send.at[2, other], head_recv.at[2, other], device(dp, z, r ^ other))
        copy.start()
        heads.append(copy)
    own = pltpu.make_async_copy(ld_vm, ld_ref.at[r], head_own.at[2])
    own.start()
    heads.append(own)

    forwards = []
    crossings = []

    def slot(k, p):
        return kv_ref.at[core, kv_rows(z - k, p)]

    def arrived(k, p):
        piece = slot(k, p)
        remote(piece, piece, first_send.at[0, 0], own_recv.at[k, p], device(dp, z, r ^ 1)).wait_recv()
        return piece

    def forward(k, p, step, piece):
        i = 0 if step > 0 else 1
        copy = remote(piece, piece, ring_send.at[i, k, p], own_recv.at[k + step, p], device(dp, z + step, r))
        copy.start()
        forwards.append(copy)

    def cross(k, p, piece):
        copy = remote(piece, piece, core_send.at[k, p], other_recv.at[k, p], device(dp, z, r ^ 1))
        copy.start()
        crossings.append((copy, k, p))

    for k in range(1, 4):
        for p in range(QUAD):
            piece = arrived(k, p)
            if k < 3 or p < 2:
                forward(k, p, 1, piece)
            cross(k, p, piece)
            piece = arrived(RING - k, p)
            if k < 3 or p >= 2:
                forward(RING - k, p, -1, piece)
            cross(RING - k, p, piece)
        if k == 1:
            for c in loads[3:]:
                c.wait()
            wanted = jnp.concatenate(
                [jnp.full((1, HD), order_sm[z * BLOCKS_HERE + block], jnp.int32) for block in range(BLOCKS_HERE)], axis=0
            )
            wanted = wanted - (WINDOW - 1) + lax.broadcasted_iota(jnp.int32, (BLOCKS_HERE, HD), 1)
            slots = lax.fori_loop(
                0, BLOCKS, lambda i, found: jnp.where(wanted == order_sm[i], i, found), jnp.zeros_like(wanted)
            )
            slot_vm[...] = slots
            to_scalars = pltpu.make_async_copy(slot_vm, slot_sm, load_sem.at[5])
            to_scalars.start()
            for p in range(QUAD):
                piece = slot(0, p)

                @pl.when(p != r)
                def _():
                    arrived(0, p)

                @pl.when(p == r)
                def _():
                    pltpu.make_async_copy(piece, piece, first_own).wait()

                cross(0, p, piece)
        if k == 2:
            within = lax.broadcasted_iota(jnp.int32, (1, LANES), 1) % HALF

            @pl.loop(0, BLOCKS_HERE)
            def _(block):
                tok_q = order_sm[z * BLOCKS_HERE + block] * HALF + within
                begin_q = jnp.zeros((1, LANES), jnp.int32)
                end = jnp.int32(0)
                for d in range(NDOC):
                    end = end + doc_sm[d]
                    begin_q = jnp.where(end <= tok_q, end, begin_q)
                begin_vm[block] = begin_q
                for kind in range(2):
                    part_vm[kind, block, 0] = jnp.zeros((HALF, HD), F32)
                    part_vm[kind, block, WINDOW + 1] = jnp.zeros((HALF, HD), F32)
    to_scalars.wait()
    for p in range(QUAD):
        cross(4, p, arrived(4, p))
    for copy, k, p in crossings:
        copy.wait_send()
        theirs = kv_ref.at[1 - core, kv_rows(z - k, p)]
        remote(theirs, theirs, core_send.at[k, p], other_recv.at[k, p], device(dp, z, r ^ 1)).wait_recv()
    for copy in heads:
        copy.wait()
    attend(z, r, qg_ref, dog_ref, kv_ref, ld_ref, order_sm, slot_sm, begin_vm, part_vm, dq_ref)
    for copy in forwards + first:
        copy.wait_send()
    for t in range(QUAD):
        @pl.when(t != r)
        def _():
            piece = slot(0, 0)
            remote(piece, piece, first_send.at[2, t], own_recv.at[0, 0], device(dp, z, r ^ 1)).wait_send()


    def shard(d):
        return rows_at(lax.rem(z + d + RING, RING) * SHARD, SHARD)

    def piece(d, p):
        return rows_at((lax.rem(z + d + RING, RING) * QUAD + p) * ROWS, ROWS)

    order = (4, 3, 5, 2, 6, 1, 7, 0)
    gifts = {}

    def combine(d):
        start = lax.rem(z + d + RING, RING) * BLOCKS_HERE

        @pl.loop(0, BLOCKS_HERE)
        def _(i):
            kb = order_sm[start + i]
            places = []
            for block in range(BLOCKS_HERE):
                at = kb - order_sm[z * BLOCKS_HERE + block] + (WINDOW - 1)
                places.append(jnp.clip(at + 1, 0, WINDOW + 1))
            rows = rows_at((start + i) * HALF, HALF)
            for out, kind in ((give_vm, 1 - core), (own_vm, core)):
                terms = [part_vm[kind, block, places[block]] for block in range(BLOCKS_HERE)]
                while len(terms) > 1:
                    terms = [x + y for x, y in zip(terms[::2], terms[1::2])]
                out[rows, :] = (terms[0] * jnp.where(kind == 0, INV_ROOT, 1.0)).astype(out.dtype)

        gifts[d] = remote(
            give_vm.at[shard(d), :], other_vm.at[shard(d), :], give_send.at[d], give_recv.at[d], device(dp, z, r ^ 1)
        )
        gifts[d].start()

    heads = []
    combine(4)
    to_cols = rows_at(r * COLS, COLS)
    for other in range(1, QUAD):
        t = r ^ other
        copy = remote(
            dq_ref.at[rows_at(t * ROWS, ROWS), :], qgrad_ref.at[:, to_cols],
            back_send.at[other], back_recv.at[other], device(dp, z, t),
        )
        copy.start()
        heads.append(copy)
    own = pltpu.make_async_copy(dq_ref.at[rows_at(r * ROWS, ROWS), :], qgrad_ref.at[:, to_cols], back_own)
    own.start()
    heads.append(own)

    def total(d, p):
        return own_vm[piece(d, p), :] + other_vm[piece(d, p), :].astype(F32)

    def ready(d):
        gifts[d].wait_recv()

    sends = []

    def pass_on(i, s, p, value):
        here = send_vm.at[i, s, p]
        here[...] = value.astype(BF16)
        copy = remote(
            here, recv_vm.at[i, s, p], sum_send.at[i, s, p], sum_recv.at[i, s, p],
            device(dp, z + (1 - 2 * i), r),
        )
        copy.start()
        sends.append(copy)

    def came(i, s, p):
        here = recv_vm.at[i, s, p]
        remote(here, here, sum_send.at[i, s, p], sum_recv.at[i, s, p], device(dp, z, r ^ 1)).wait_recv()
        return here[...].astype(F32)

    first_half, second_half = (0, 1), (2, 3)
    combine(3)
    combine(5)
    ready(4)
    for a, b in zip(first_half, second_half):
        pass_on(0, 0, a, total(4, a))
        pass_on(1, 0, b, total(4, b))
    ready(3)
    ready(5)
    for a, b in zip(second_half, first_half):
        pass_on(0, 1, a, total(3, a))
        pass_on(1, 1, b, total(5, b))
    combine(2)
    combine(6)
    for a, b in zip(first_half, second_half):
        pass_on(0, 1, a, total(3, a) + came(0, 0, a))
        pass_on(1, 1, b, total(5, b) + came(1, 0, b))
    combine(1)
    combine(7)
    combine(0)
    ready(2)
    ready(6)
    for a, b in zip(second_half + first_half, first_half + second_half):
        pass_on(0, 2, a, total(2, a) + came(0, 1, a))
        pass_on(1, 2, b, total(6, b) + came(1, 1, b))
    ready(1)
    ready(7)
    ready(0)

    def finish(i, d, p, value):
        here = last_vm.at[i, p]
        here[...] = value.astype(BF16)
        there = final_vm.at[i, r]
        copy = remote(here, there, last_send.at[i, p], last_recv.at[i, r], device(dp, z + d, p))
        if d:
            copy.start()
            sends.append(copy)
        else:
            @pl.when(p != r)
            def _():
                copy.start()

            @pl.when(p == r)
            def _():
                there[...] = here[...]

    for p in range(QUAD):
        finish(2, 0, p, total(0, p))
    for a, b in zip(second_half + first_half, first_half + second_half):
        finish(0, 1, a, total(1, a) + came(0, 2, a))
        finish(1, -1, b, total(7, b) + came(1, 2, b))
    for t in range(QUAD):
        for i in range(3):
            here = final_vm.at[i, t]
            arrival = remote(here, here, last_send.at[i, t], last_recv.at[i, t], device(dp, z, r ^ 1))
            if i < 2:
                arrival.wait_recv()
            else:
                @pl.when(t != r)
                def _():
                    arrival.wait_recv()
        value = final_vm[0, t].astype(F32) + final_vm[1, t].astype(F32) + final_vm[2, t].astype(F32)
        out = vgrad_ref if t % 2 else kgrad_ref
        out[:, (t // 2) * HD : (t // 2 + 1) * HD] = value.astype(BF16)
    for p in range(QUAD):
        @pl.when(p != r)
        def _():
            here = last_vm.at[2, p]
            remote(here, here, last_send.at[2, p], last_recv.at[2, p], device(dp, z, r ^ 1)).wait_send()
    for copy in sends:
        copy.wait_send()
    for d in order:
        gifts[d].wait_send()
    for copy in heads:
        copy.wait()


ANY = pl.BlockSpec(memory_space=pl.ANY)
VMEM = pl.BlockSpec(memory_space=pltpu.VMEM)
DMA = pltpu.SemaphoreType.DMA
LIMIT = 60


def local(query, keys, values, attn_out, grad_out, log_total, doc_lengths, block_order):
    return pl.pallas_call(
        kernel,
        out_shape=(
            jax.ShapeDtypeStruct((ROWS, HEADS * HD), BF16),
            jax.ShapeDtypeStruct((ROWS, GROUPS * HD), BF16),
            jax.ShapeDtypeStruct((ROWS, GROUPS * HD), BF16),
        ),
        in_specs=[ANY] * 8,
        out_specs=(ANY, VMEM, VMEM),
        scratch_shapes=[
            pltpu.VMEM((ROWS, HEADS * HD), BF16),
            pltpu.VMEM((ROWS, HEADS * HD), BF16),
            pltpu.VMEM((2, GROUPS, 2, HALF, HD), BF16),
            pltpu.VMEM((HEADS, ROWS), F32),
            pltpu.VMEM((2, 2, QUAD, LANES), F32),
            pltpu.VMEM((SHARD, COLS), BF16),
            pltpu.VMEM((SHARD, COLS), BF16),
            pltpu.VMEM((2, BLOCKS, HALF, HD), BF16),
            pltpu.VMEM((QUAD, 2, 2, QUAD, LANES), F32),
            pltpu.SMEM((NDOC,), jnp.int32),
            pltpu.SMEM((BLOCKS,), jnp.int32),
            pltpu.VMEM((BLOCKS_HERE, HD), jnp.int32),
            pltpu.SMEM((BLOCKS_HERE, HD), jnp.int32),
            pltpu.VMEM((BLOCKS_HERE, 1, LANES), jnp.int32),
            pltpu.VMEM((2, BLOCKS_HERE, WINDOW + 2, HALF, HD), F32),
            pltpu.VMEM((SHARD, COLS), BF16),
            pltpu.VMEM((SEQ, HD), F32),
            pltpu.VMEM((SEQ, HD), BF16),
            pltpu.VMEM((SEQ, HD), BF16),
            pltpu.VMEM((2, 3, QUAD, ROWS, HD), BF16),
            pltpu.VMEM((2, 3, QUAD, ROWS, HD), BF16),
            pltpu.VMEM((3, QUAD, ROWS, HD), BF16),
            pltpu.VMEM((3, QUAD, ROWS, HD), BF16),
            DMA((6,)),
            DMA((8,)),
            DMA((3, QUAD)),
            DMA,
            DMA((RING, QUAD)),
            DMA((RING, QUAD)),
            DMA((2, RING, QUAD)),
            DMA((RING, QUAD)),
            DMA((3, QUAD)),
            DMA((3, QUAD)),
            DMA((3,)),
            DMA((RING,)),
            DMA((RING,)),
            DMA((2, 3, QUAD)),
            DMA((2, 3, QUAD)),
            DMA((3, QUAD)),
            DMA((3, QUAD)),
            DMA((QUAD,)),
            DMA((QUAD,)),
            DMA,
        ],
        compiler_params=pltpu.CompilerParams(
            collective_id=0, has_side_effects=True, vmem_limit_bytes=LIMIT * 2**20
        ),
    )(query, keys, values, attn_out, grad_out, log_total, doc_lengths, block_order)


def solution(mesh):
    rows = P(("dp", "ctx"), None)
    return jax.shard_map(
        local,
        mesh=mesh,
        in_specs=(rows, rows, rows, rows, rows, P(None, ("dp", "ctx")), P("dp"), P("dp")),
        out_specs=(rows, rows, rows),
        check_vma=False,
    )
```

time: 69 us -> 62 us (0.90); the launches traced: 68 us -> 61.9 us
  local copies, waits for them, and re-layouts: 8.85 us -> 3.41 us
  Pallas kernels: 58.5 us -> 57.8 us
    unnamed x19 -> x7, local copies, waits for them, and re-layouts: 8.85 us -> 3.41 us
    pallas_call x3 -> x1, Pallas kernels: 58.5 us -> 57.8 us  [local(): pl.pallas_call(kernel, out_shape=(jax.ShapeDtypeStruct((ROWS, HEADS * HD)...]
where the time goes in v2:
time: 62 us; the launch traced here: 61.9 us
  Pallas kernels  57.8 us (93%)
  local copies, waits for them, and re-layouts  3.41 us (6%)
  between operations  0.65 us (1%)
    pallas_call x1, Pallas kernels, local(): pl.pallas_call(kernel, out_shape=(jax.ShapeDtypeStruct((ROWS, HEADS * HD)...  57.8 us
    unnamed x7, local copies, waits for them, and re-layouts  3.41 us

profile of v2, /device:TPU:1, one launch (start us, length us, event | category | flops | bytes accessed | tf_op | source)
XLA Modules:
  0.0 61.9 jit_solution(17957979746067262437)
XLA Ops:
  0.6 57.8 %shard_map.103 = (bf16[128,2048]{1,0:T(8,128)(2,1)}, bf16[128,256]{1,0:T(8,128)(2,1)}, bf16[128,256]{1,0:T(8,128)(2,1)}) custom-call(bf16[128,2048]{1,0:T(8,128)(2,1)} %q_ref.1, bf16[128,256]{1,0:T(8,128)(2,1)} %k_ref.1, bf16[128,256]{1,0:T(8,128)(2,1)} %v_ref.1, bf16[128,2048]{1,0:T(8,128)(2,1)} %o_ref.1, bf16[128,2048]{1,0:T(8,128)(2,1)} %do_ref.1, ...), custom_call_target="tpu_custom_call" | custom-call | tf_op jit(solution)/shard_map/pallas_call | solution.py:446
  58.5 0.0 copy-start.1
  58.5 1.9 %copy.14 = bf16[128,2048]{1,0:T(8,128)(2,1)} copy(bf16[128,2048]{1,0:T(8,128)(2,1)} %get-tuple-element.6) | data formatting | bytes 1048576
  60.4 0.0 copy-done.1
  60.4 0.0 copy-start
  60.4 0.6 %copy.15 = bf16[128,256]{1,0:T(8,128)(2,1)} copy(bf16[128,256]{1,0:T(8,128)(2,1)S(1)} %copy-done.1) | data formatting | bytes 131072
  61.0 0.2 copy-done
  61.2 0.6 %copy.16 = bf16[128,256]{1,0:T(8,128)(2,1)} copy(bf16[128,256]{1,0:T(8,128)(2,1)S(1)} %copy-done) | data formatting | bytes 131072
Async XLA Ops:
  58.5 1.9 %copy-start.1 = (bf16[128,256]{1,0:T(8,128)(2,1)S(1)}, bf16[128,256]{1,0:T(8,128)(2,1)}, u32[]{:S(2)}) copy-start(bf16[128,256]{1,0:T(8,128)(2,1)} %get-tuple-element.7) | copy-start | bytes 196612
  60.4 0.9 %copy-start = (bf16[128,256]{1,0:T(8,128)(2,1)S(1)}, bf16[128,256]{1,0:T(8,128)(2,1)}, u32[]{:S(2)}) copy-start(bf16[128,256]{1,0:T(8,128)(2,1)} %get-tuple-element.8) | copy-start | bytes 196612

commit v3 on v2

--- a/solution.py
+++ b/solution.py
@@ -75,9 +75,14 @@
     return lax.dot_general(a, b, (((1,), (1,)), ((), ())), preferred_element_type=F32)
 
 
-def attend(z, r, qg_ref, dog_ref, kv_ref, ld_ref, order_sm, slot_sm, begin_vm, part_vm, dq_ref):
+def attend(z, r, qg_ref, dog_ref, kv_ref, ld_ref, order_sm, slot_sm, begin_vm, part_vm, ds_vm, wait_far):
     @pl.loop(0, BLOCKS_HERE)
-    def _(block):
+    def _(i):
+        @pl.when(i == BLOCKS_HERE // 2)
+        def _():
+            wait_far()
+
+        block = lax.rem(i + (r // 2) * (BLOCKS_HERE // 2), BLOCKS_HERE)
         b = order_sm[z * BLOCKS_HERE + block]
         tok_q = b * HALF + lax.broadcasted_iota(jnp.int32, (1, LANES), 1) % HALF
         begin_q = begin_vm[block]
@@ -86,7 +91,6 @@
         do = jnp.concatenate([dog_ref[rows, e * HD : (e + 1) * HD] for e in range(MEMBER_HEADS)], axis=0)
         lse = ld_ref[block // 2, 0, lax.rem(block, 2), pl.ds(r, 1), :]
         delta = ld_ref[block // 2, 1, lax.rem(block, 2), pl.ds(r, 1), :]
-        dqt = jnp.zeros((HD, LANES), F32)
         for first, last in TILES:
             base = b - (WINDOW - 1) + first
             places = [slot_sm[block, j] for j in range(first, last)]
@@ -103,19 +107,16 @@
             blocks = (last - first, HALF, HD)
             part_vm[1, block, there] = jnp.dot(probs_low, do, preferred_element_type=F32).reshape(blocks)
             part_vm[0, block, there] = jnp.dot(dscore, q, preferred_element_type=F32).reshape(blocks)
-            dqt += lax.dot_general(k, dscore, (((0,), (0,)), ((), ())), preferred_element_type=F32)
-        dq = (dqt.T * INV_ROOT).astype(BF16)
-        for e in range(MEMBER_HEADS):
-            dq_ref[rows, e * HD : (e + 1) * HD] = dq[e * HALF : (e + 1) * HALF]
+            ds_vm[block, first * HALF : last * HALF, :] = dscore
 
 
 def kernel(
     q_ref, k_ref, v_ref, o_ref, do_ref, lse_ref, doc_ref, order_ref,
     qgrad_ref, kgrad_ref, vgrad_ref,
     o_vm, do_vm, own_kv, lse_vm, ld_vm, qg_ref, dog_ref, kv_ref, ld_ref,
-    doc_sm, order_sm, slot_vm, slot_sm, begin_vm, part_vm, dq_ref,
+    doc_sm, order_sm, slot_vm, slot_sm, begin_vm, part_vm, ds_vm, dq_ref,
     own_vm, give_vm, other_vm, recv_vm, send_vm, last_vm, final_vm,
-    load_sem, own_sem, first_send, first_own, own_recv, other_recv, ring_send, core_send, head_send, head_recv, head_own,
+    load_sem, own_sem, first_send, first_own, first_recv, half_recv, other_recv, ring_send, core_send, head_send, head_recv, head_own,
     give_send, give_recv, sum_send, sum_recv, last_send, last_recv, back_send, back_recv, back_own,
 ):
     dp, z, r = place()
@@ -163,8 +164,8 @@
         for t in range(QUAD):
             source = own_kv.at[t % 2, t // 2]
             target = kv_ref.at[t % 2, mine]
-            copy = remote(source, target, first_send.at[i, t], own_recv.at[dz % RING, r], device(dp, z + dz, t))
-            if dz:
+            copy = remote(source, target, first_send.at[i, t], first_recv.at[i, r], device(dp, z + dz, t))
+            if i != 2:
                 copy.start()
                 first.append(copy)
             else:
@@ -176,7 +177,8 @@
                 def _():
                     pltpu.make_async_copy(source, target, first_own).start()
 
-    heads = []
+    near_heads = []
+    far_heads = []
     for i, (src, dst) in enumerate(((q_ref, qg_ref), (do_ref, dog_ref))):
         to_rows = rows_at(r * ROWS, ROWS)
         for other in range(1, QUAD):
@@ -186,115 +188,142 @@
                 src.at[:, cols], dst.at[to_rows, :], head_send.at[i, other], head_recv.at[i, other], device(dp, z, t)
             )
             copy.start()
-            heads.append(copy)
+            (near_heads if other == 1 else far_heads).append(copy)
         own = pltpu.make_async_copy(src.at[:, rows_at(r * COLS, COLS)], dst.at[to_rows, :], head_own.at[i])
         own.start()
-        heads.append(own)
+        near_heads.append(own)
 
     for other in range(1, QUAD):
         copy = remote(ld_vm, ld_ref.at[r], head_send.at[2, other], head_recv.at[2, other], device(dp, z, r ^ other))
         copy.start()
-        heads.append(copy)
+        (near_heads if other == 1 else far_heads).append(copy)
     own = pltpu.make_async_copy(ld_vm, ld_ref.at[r], head_own.at[2])
     own.start()
-    heads.append(own)
+    near_heads.append(own)
 
     forwards = []
     crossings = []
 
-    def slot(k, p):
-        return kv_ref.at[core, kv_rows(z - k, p)]
-
-    def arrived(k, p):
-        piece = slot(k, p)
-        remote(piece, piece, first_send.at[0, 0], own_recv.at[k, p], device(dp, z, r ^ 1)).wait_recv()
-        return piece
-
-    def forward(k, p, step, piece):
-        i = 0 if step > 0 else 1
-        copy = remote(piece, piece, ring_send.at[i, k, p], own_recv.at[k + step, p], device(dp, z + step, r))
+    def half_of(k, h):
+        return kv_ref.at[core, pl.ds((lax.rem(z - k + RING, RING) * 2 + h) * QUAD, QUAD)]
+
+    def first_arrived(i, pieces):
+        for p in pieces:
+            there = kv_ref.at[core, kv_rows(z, p)]
+            arrival = remote(there, there, first_send.at[i, 0], first_recv.at[i, p], device(dp, z, r ^ 1))
+            if i < 2:
+                arrival.wait_recv()
+            else:
+                @pl.when(p != r)
+                def _():
+                    arrival.wait_recv()
+
+                @pl.when(p == r)
+                def _():
+                    pltpu.make_async_copy(there, there, first_own).wait()
+
+    def arrived(k, h):
+        there = half_of(k, h)
+        remote(there, there, ring_send.at[0, k, h], half_recv.at[k, h], device(dp, z, r ^ 1)).wait_recv()
+
+    def forward(i, k, h):
+        step = 1 - 2 * i
+        there = half_of(k, h)
+        copy = remote(there, there, ring_send.at[i, k, h], half_recv.at[k + step, h], device(dp, z + step, r))
         copy.start()
         forwards.append(copy)
 
-    def cross(k, p, piece):
-        copy = remote(piece, piece, core_send.at[k, p], other_recv.at[k, p], device(dp, z, r ^ 1))
+    def crossed(kind, k, h=None):
+        zk = lax.rem(z - k + RING, RING)
+        if h is None:
+            there = kv_ref.at[kind, pl.ds(zk * BLOCKS_HERE, BLOCKS_HERE)]
+        else:
+            there = kv_ref.at[kind, pl.ds((zk * 2 + h) * QUAD, QUAD)]
+        at = k if not h else RING
+        return remote(there, there, core_send.at[at], other_recv.at[at], device(dp, z, r ^ 1))
+
+    def cross(k, h=None):
+        copy = crossed(core, k, h)
         copy.start()
-        crossings.append((copy, k, p))
-
-    for k in range(1, 4):
-        for p in range(QUAD):
-            piece = arrived(k, p)
-            if k < 3 or p < 2:
-                forward(k, p, 1, piece)
-            cross(k, p, piece)
-            piece = arrived(RING - k, p)
-            if k < 3 or p >= 2:
-                forward(RING - k, p, -1, piece)
-            cross(RING - k, p, piece)
-        if k == 1:
-            for c in loads[3:]:
-                c.wait()
-            wanted = jnp.concatenate(
-                [jnp.full((1, HD), order_sm[z * BLOCKS_HERE + block], jnp.int32) for block in range(BLOCKS_HERE)], axis=0
-            )
-            wanted = wanted - (WINDOW - 1) + lax.broadcasted_iota(jnp.int32, (BLOCKS_HERE, HD), 1)
-            slots = lax.fori_loop(
-                0, BLOCKS, lambda i, found: jnp.where(wanted == order_sm[i], i, found), jnp.zeros_like(wanted)
-            )
-            slot_vm[...] = slots
-            to_scalars = pltpu.make_async_copy(slot_vm, slot_sm, load_sem.at[5])
-            to_scalars.start()
-            for p in range(QUAD):
-                piece = slot(0, p)
-
-                @pl.when(p != r)
-                def _():
-                    arrived(0, p)
-
-                @pl.when(p == r)
-                def _():
-                    pltpu.make_async_copy(piece, piece, first_own).wait()
-
-                cross(0, p, piece)
-        if k == 2:
-            within = lax.broadcasted_iota(jnp.int32, (1, LANES), 1) % HALF
-
-            @pl.loop(0, BLOCKS_HERE)
-            def _(block):
-                tok_q = order_sm[z * BLOCKS_HERE + block] * HALF + within
-                begin_q = jnp.zeros((1, LANES), jnp.int32)
-                end = jnp.int32(0)
-                for d in range(NDOC):
-                    end = end + doc_sm[d]
-                    begin_q = jnp.where(end <= tok_q, end, begin_q)
-                begin_vm[block] = begin_q
-                for kind in range(2):
-                    part_vm[kind, block, 0] = jnp.zeros((HALF, HD), F32)
-                    part_vm[kind, block, WINDOW + 1] = jnp.zeros((HALF, HD), F32)
+        crossings.append((copy, k, h))
+
+    for h in range(2):
+        for i, hi in ((0, h), (1, 1 - h)):
+            first_arrived(i, (2 * hi, 2 * hi + 1))
+            forward(i, 1 if i == 0 else RING - 1, hi)
+    cross(1)
+    cross(RING - 1)
+    first_arrived(2, range(QUAD))
+    cross(0)
+    for c in loads[3:]:
+        c.wait()
+    wanted = jnp.concatenate(
+        [jnp.full((1, HD), order_sm[z * BLOCKS_HERE + block], jnp.int32) for block in range(BLOCKS_HERE)], axis=0
+    )
+    wanted = wanted - (WINDOW - 1) + lax.broadcasted_iota(jnp.int32, (BLOCKS_HERE, HD), 1)
+    slots = lax.fori_loop(
+        0, BLOCKS, lambda i, found: jnp.where(wanted == order_sm[i], i, found), jnp.zeros_like(wanted)
+    )
+    slot_vm[...] = slots
+    to_scalars = pltpu.make_async_copy(slot_vm, slot_sm, load_sem.at[5])
+    to_scalars.start()
+    for h in range(2):
+        for i, k, hi in ((0, 2, h), (1, RING - 2, 1 - h)):
+            arrived(k, hi)
+            forward(i, k, hi)
+    cross(2)
+    cross(RING - 2)
+    within = lax.broadcasted_iota(jnp.int32, (1, LANES), 1) % HALF
+
+    @pl.loop(0, BLOCKS_HERE)
+    def _(block):
+        tok_q = order_sm[z * BLOCKS_HERE + block] * HALF + within
+        begin_q = jnp.zeros((1, LANES), jnp.int32)
+        end = jnp.int32(0)
+        for d in range(NDOC):
+            end = end + doc_sm[d]
+            begin_q = jnp.where(end <= tok_q, end, begin_q)
+        begin_vm[block] = begin_q
+        for kind in range(2):
+            part_vm[kind, block, 0] = jnp.zeros((HALF, HD), F32)
+            part_vm[kind, block, WINDOW + 1] = jnp.zeros((HALF, HD), F32)
     to_scalars.wait()
-    for p in range(QUAD):
-        cross(4, p, arrived(4, p))
-    for copy, k, p in crossings:
-        copy.wait_send()
-        theirs = kv_ref.at[1 - core, kv_rows(z - k, p)]
-        remote(theirs, theirs, core_send.at[k, p], other_recv.at[k, p], device(dp, z, r ^ 1)).wait_recv()
-    for copy in heads:
+    for h in range(2):
+        for i, k, hi in ((0, 3, h), (1, RING - 3, 1 - h)):
+            arrived(k, hi)
+            if h == 0:
+                forward(i, k, hi)
+    cross(3)
+    cross(RING - 3)
+    for h in range(2):
+        arrived(4, h)
+        cross(4, h)
+    for _, k, h in crossings:
+        crossed(1 - core, k, h).wait_recv()
+    for copy in near_heads:
         copy.wait()
-    attend(z, r, qg_ref, dog_ref, kv_ref, ld_ref, order_sm, slot_sm, begin_vm, part_vm, dq_ref)
-    for copy in forwards + first:
-        copy.wait_send()
-    for t in range(QUAD):
-        @pl.when(t != r)
-        def _():
-            piece = slot(0, 0)
-            remote(piece, piece, first_send.at[2, t], own_recv.at[0, 0], device(dp, z, r ^ 1)).wait_send()
-
+
+    def wait_far_heads():
+        for copy in far_heads:
+            copy.wait()
+
+    attend(z, r, qg_ref, dog_ref, kv_ref, ld_ref, order_sm, slot_sm, begin_vm, part_vm, ds_vm, wait_far_heads)
+    def settle():
+        for copy, _, _ in crossings:
+            copy.wait_send()
+        for copy in forwards + first:
+            copy.wait_send()
+        for t in range(QUAD):
+            @pl.when(t != r)
+            def _():
+                there = kv_ref.at[0, kv_rows(z, 0)]
+                remote(there, there, first_send.at[2, t], first_recv.at[2, 0], device(dp, z, r ^ 1)).wait_send()
 
     def shard(d):
         return rows_at(lax.rem(z + d + RING, RING) * SHARD, SHARD)
 
     def piece(d, p):
-        return rows_at((lax.rem(z + d + RING, RING) * QUAD + p) * ROWS, ROWS)
+        return rows_at((lax.rem(z + d + RING, RING) * 2 + p) * ROWS * 2, ROWS * 2)
 
     order = (4, 3, 5, 2, 6, 1, 7, 0)
     gifts = {}
@@ -322,9 +351,19 @@
         gifts[d].start()
 
     heads = []
-    combine(4)
     to_cols = rows_at(r * COLS, COLS)
-    for other in range(1, QUAD):
+
+    def query_terms(first_member):
+        @pl.loop(0, BLOCKS_HERE // 2)
+        def _(i):
+            block = first_member * 2 + i
+            k = jnp.concatenate([kv_ref[0, slot_sm[block, j]] for j in range(WINDOW)], axis=0)
+            dqt = lax.dot_general(k, ds_vm[block], (((0,), (0,)), ((), ())), preferred_element_type=F32)
+            dq = (dqt.T * (INV_ROOT * 0.5)).astype(BF16)
+            for e in range(MEMBER_HEADS):
+                dq_ref[rows_at(block * HALF, HALF), e * HD : (e + 1) * HD] = dq[e * HALF : (e + 1) * HALF]
+
+    def send_back(other):
         t = r ^ other
         copy = remote(
             dq_ref.at[rows_at(t * ROWS, ROWS), :], qgrad_ref.at[:, to_cols],
@@ -332,9 +371,6 @@
         )
         copy.start()
         heads.append(copy)
-    own = pltpu.make_async_copy(dq_ref.at[rows_at(r * ROWS, ROWS), :], qgrad_ref.at[:, to_cols], back_own)
-    own.start()
-    heads.append(own)
 
     def total(d, p):
         return own_vm[piece(d, p), :] + other_vm[piece(d, p), :].astype(F32)
@@ -359,70 +395,77 @@
         remote(here, here, sum_send.at[i, s, p], sum_recv.at[i, s, p], device(dp, z, r ^ 1)).wait_recv()
         return here[...].astype(F32)
 
-    first_half, second_half = (0, 1), (2, 3)
+    combine(4)
     combine(3)
     combine(5)
     ready(4)
-    for a, b in zip(first_half, second_half):
-        pass_on(0, 0, a, total(4, a))
-        pass_on(1, 0, b, total(4, b))
+    pass_on(0, 0, 0, total(4, 0))
+    pass_on(1, 0, 1, total(4, 1))
     ready(3)
     ready(5)
-    for a, b in zip(second_half, first_half):
-        pass_on(0, 1, a, total(3, a))
-        pass_on(1, 1, b, total(5, b))
+    pass_on(0, 1, 1, total(3, 1))
+    pass_on(1, 1, 0, total(5, 0))
     combine(2)
     combine(6)
-    for a, b in zip(first_half, second_half):
-        pass_on(0, 1, a, total(3, a) + came(0, 0, a))
-        pass_on(1, 1, b, total(5, b) + came(1, 0, b))
+    query_terms((1 - r // 2) * 2)
+    send_back(2)
+    send_back(3)
+    pass_on(0, 1, 0, total(3, 0) + came(0, 0, 0))
+    pass_on(1, 1, 1, total(5, 1) + came(1, 0, 1))
+    ready(2)
+    ready(6)
+    for h in range(2):
+        pass_on(0, 2, 1 - h, total(2, 1 - h) + came(0, 1, 1 - h))
+        pass_on(1, 2, h, total(6, h) + came(1, 1, h))
     combine(1)
     combine(7)
     combine(0)
-    ready(2)
-    ready(6)
-    for a, b in zip(second_half + first_half, first_half + second_half):
-        pass_on(0, 2, a, total(2, a) + came(0, 1, a))
-        pass_on(1, 2, b, total(6, b) + came(1, 1, b))
+    query_terms((r // 2) * 2)
+    send_back(1)
+    own = pltpu.make_async_copy(dq_ref.at[rows_at(r * ROWS, ROWS), :], qgrad_ref.at[:, to_cols], back_own)
+    own.start()
+    heads.append(own)
     ready(1)
     ready(7)
     ready(0)
 
-    def finish(i, d, p, value):
-        here = last_vm.at[i, p]
-        here[...] = value.astype(BF16)
-        there = final_vm.at[i, r]
-        copy = remote(here, there, last_send.at[i, p], last_recv.at[i, r], device(dp, z + d, p))
-        if d:
-            copy.start()
-            sends.append(copy)
-        else:
-            @pl.when(p != r)
-            def _():
+    def finish(i, d, h, value):
+        for p in (2 * h, 2 * h + 1):
+            here = last_vm.at[i, p]
+            here[...] = value[(p - 2 * h) * ROWS : (p - 2 * h + 1) * ROWS].astype(BF16)
+            there = final_vm.at[i, r]
+            copy = remote(here, there, last_send.at[i, p], last_recv.at[i, r], device(dp, z + d, p))
+            if d:
                 copy.start()
-
-            @pl.when(p == r)
-            def _():
-                there[...] = here[...]
-
-    for p in range(QUAD):
-        finish(2, 0, p, total(0, p))
-    for a, b in zip(second_half + first_half, first_half + second_half):
-        finish(0, 1, a, total(1, a) + came(0, 2, a))
-        finish(1, -1, b, total(7, b) + came(1, 2, b))
+                sends.append(copy)
+            else:
+                @pl.when(p != r)
+                def _():
+                    copy.start()
+
+                @pl.when(p == r)
+                def _():
+                    there[...] = here[...]
+
+    for h in range(2):
+        finish(2, 0, h, total(0, h))
+    settle()
+    for h in range(2):
+        finish(0, 1, 1 - h, total(1, 1 - h) + came(0, 2, 1 - h))
+        finish(1, -1, h, total(7, h) + came(1, 2, h))
     for t in range(QUAD):
-        for i in range(3):
+        for i in (2, 0, 1):
             here = final_vm.at[i, t]
             arrival = remote(here, here, last_send.at[i, t], last_recv.at[i, t], device(dp, z, r ^ 1))
-            if i < 2:
+            if i != 2:
                 arrival.wait_recv()
             else:
                 @pl.when(t != r)
                 def _():
                     arrival.wait_recv()
-        value = final_vm[0, t].astype(F32) + final_vm[1, t].astype(F32) + final_vm[2, t].astype(F32)
+        value = sum(final_vm[i, t].astype(F32) for i in range(3))
         out = vgrad_ref if t % 2 else kgrad_ref
-        out[:, (t // 2) * HD : (t // 2 + 1) * HD] = value.astype(BF16)
+        out[:, (t // 2) * HD : (t // 2 + 1) * HD] = (value * 0.5).astype(BF16)
     for p in range(QUAD):
         @pl.when(p != r)
         def _():
@@ -443,7 +486,7 @@
 
 
 def local(query, keys, values, attn_out, grad_out, log_total, doc_lengths, block_order):
-    return pl.pallas_call(
+    halves = pl.pallas_call(
         kernel,
         out_shape=(
             jax.ShapeDtypeStruct((ROWS, HEADS * HD), BF16),
@@ -468,29 +511,31 @@
             pltpu.SMEM((BLOCKS_HERE, HD), jnp.int32),
             pltpu.VMEM((BLOCKS_HERE, 1, LANES), jnp.int32),
             pltpu.VMEM((2, BLOCKS_HERE, WINDOW + 2, HALF, HD), F32),
+            pltpu.VMEM((BLOCKS_HERE, WINDOW * HALF, LANES), BF16),
             pltpu.VMEM((SHARD, COLS), BF16),
             pltpu.VMEM((SEQ, HD), F32),
             pltpu.VMEM((SEQ, HD), BF16),
             pltpu.VMEM((SEQ, HD), BF16),
-            pltpu.VMEM((2, 3, QUAD, ROWS, HD), BF16),
-            pltpu.VMEM((2, 3, QUAD, ROWS, HD), BF16),
+            pltpu.VMEM((2, 3, 2, 2 * ROWS, HD), BF16),
+            pltpu.VMEM((2, 3, 2, 2 * ROWS, HD), BF16),
             pltpu.VMEM((3, QUAD, ROWS, HD), BF16),
             pltpu.VMEM((3, QUAD, ROWS, HD), BF16),
             DMA((6,)),
             DMA((8,)),
             DMA((3, QUAD)),
             DMA,
-            DMA((RING, QUAD)),
-            DMA((RING, QUAD)),
-            DMA((2, RING, QUAD)),
-            DMA((RING, QUAD)),
+            DMA((3, QUAD)),
+            DMA((RING, 2)),
+            DMA((RING + 1,)),
+            DMA((2, RING, 2)),
+            DMA((RING + 1,)),
             DMA((3, QUAD)),
             DMA((3, QUAD)),
             DMA((3,)),
             DMA((RING,)),
             DMA((RING,)),
-            DMA((2, 3, QUAD)),
-            DMA((2, 3, QUAD)),
+            DMA((2, 3, 2)),
+            DMA((2, 3, 2)),
             DMA((3, QUAD)),
             DMA((3, QUAD)),
             DMA((QUAD,)),
@@ -501,6 +546,7 @@
             collective_id=0, has_side_effects=True, vmem_limit_bytes=LIMIT * 2**20
         ),
     )(query, keys, values, attn_out, grad_out, log_total, doc_lengths, block_order)
+    return tuple(half * 2 for half in halves)
 
 
 def solution(mesh):

time: 62 us -> 60.5 us (0.976)
  local copies, waits for them, and re-layouts: 3.41 us -> 0.01 us
  other arithmetic: 0 us -> 2.57 us
  Pallas kernels: 57.8 us -> 57.1 us
    unnamed x7 -> x4, local copies, waits for them, and re-layouts: 3.41 us -> 0.01 us
    mul x0 -> x2, other arithmetic: none -> 2.57 us  [local(): return tuple((half * 2 for half in halves))]
    pallas_call x1, Pallas kernels: 57.8 us -> 57.1 us  [local(): pl.pallas_call(kernel, out_shape=(jax.ShapeDtypeStruct((ROWS, HEADS * HD)...]
where the time goes in v3:
time: 60.5 us; the launch traced here: 60.3 us
  Pallas kernels  57.1 us (94%)
  other arithmetic  2.57 us (4%)
  between operations  0.66 us (1%)
    pallas_call x1, Pallas kernels, local(): pl.pallas_call(kernel, out_shape=(jax.ShapeDtypeStruct((ROWS, HEADS * HD)...  57.1 us
    mul x2, other arithmetic, local(): return tuple((half * 2 for half in halves))  2.57 us

profile of v3, /device:TPU:1, one launch (start us, length us, event | category | flops | bytes accessed | tf_op | source)
XLA Modules:
  0.0 60.3 jit_solution(2406264932998053753)
XLA Ops:
  0.6 57.1 %shard_map.103 = (bf16[128,2048]{1,0:T(8,128)(2,1)}, bf16[128,256]{1,0:T(8,128)(2,1)}, bf16[128,256]{1,0:T(8,128)(2,1)}) custom-call(bf16[128,2048]{1,0:T(8,128)(2,1)} %q_ref.1, bf16[128,256]{1,0:T(8,128)(2,1)} %k_ref.1, bf16[128,256]{1,0:T(8,128)(2,1)} %v_ref.1, bf16[128,2048]{1,0:T(8,128)(2,1)} %o_ref.1, bf16[128,2048]{1,0:T(8,128)(2,1)} %do_ref.1, ...), custom_call_target="tpu_custom_call" | custom-call | tf_op jit(solution)/shard_map/pallas_call | solution.py:489
  57.8 0.0 copy-start
  57.8 0.0 copy-start.1
  57.8 1.9 %broadcast_multiply_fusion = bf16[128,2048]{1,0:T(8,128)(2,1)} fusion(bf16[128,2048]{1,0:T(8,128)(2,1)} %get-tuple-element.6), kind=kLoop, calls=%fused_computation | loop fusion | flops 262144 | bytes 1048576 | tf_op jit(solution)/shard_map/mul | solution.py:549
  59.7 0.0 copy-done
  59.7 0.0 copy-done.1
  59.7 0.7 %broadcast_multiply_fusion.1 = (bf16[128,256]{1,0:T(8,128)(2,1)}, bf16[128,256]{1,0:T(8,128)(2,1)}) fusion(bf16[128,256]{1,0:T(8,128)(2,1)S(1)} %copy-done.1, bf16[128,256]{1,0:T(8,128)(2,1)S(1)} %copy-done), kind=kLoop, calls=%fused_computation.1 | loop fusion | flops 65536 | bytes 262144 | tf_op jit(solution)/shard_map/mul | solution.py:549
Async XLA Ops:
  57.8 1.9 %copy-start = (bf16[128,256]{1,0:T(8,128)(2,1)S(1)}, bf16[128,256]{1,0:T(8,128)(2,1)}, u32[]{:S(2)}) copy-start(bf16[128,256]{1,0:T(8,128)(2,1)} %get-tuple-element.7) | copy-start | bytes 196612
  57.8 1.9 %copy-start.1 = (bf16[128,256]{1,0:T(8,128)(2,1)S(1)}, bf16[128,256]{1,0:T(8,128)(2,1)}, u32[]{:S(2)}) copy-start(bf16[128,256]{1,0:T(8,128)(2,1)} %get-tuple-element.8) | copy-start | bytes 196612

commit v4 on v3

--- a/solution.py
+++ b/solution.py
@@ -115,9 +115,9 @@
     qgrad_ref, kgrad_ref, vgrad_ref,
     o_vm, do_vm, own_kv, lse_vm, ld_vm, qg_ref, dog_ref, kv_ref, ld_ref,
     doc_sm, order_sm, slot_vm, slot_sm, begin_vm, part_vm, ds_vm, dq_ref,
-    own_vm, give_vm, other_vm, recv_vm, send_vm, last_vm, final_vm,
+    own_vm, give_vm, other_vm, extra_vm, recv_vm, send_vm, last_vm, final_vm,
     load_sem, own_sem, first_send, first_own, first_recv, half_recv, other_recv, ring_send, core_send, head_send, head_recv, head_own,
-    give_send, give_recv, sum_send, sum_recv, last_send, last_recv, back_send, back_recv, back_own,
+    give_send, give_recv, extra_send, extra_recv, sum_send, sum_recv, last_send, last_recv, back_send, back_recv, back_own,
 ):
     dp, z, r = place()
     core = lax.rem(r, 2)
@@ -331,7 +331,7 @@
     def combine(d):
         start = lax.rem(z + d + RING, RING) * BLOCKS_HERE
 
-        @pl.loop(0, BLOCKS_HERE)
+        @pl.loop(0, BLOCKS_HERE, unroll=2)
         def _(i):
             kb = order_sm[start + i]
             places = []
@@ -345,6 +345,8 @@
                     terms = [x + y for x, y in zip(terms[::2], terms[1::2])]
                 out[rows, :] = (terms[0] * jnp.where(kind == 0, INV_ROOT, 1.0)).astype(out.dtype)
 
+        if d == 4:
+            return
         gifts[d] = remote(
             give_vm.at[shard(d), :], other_vm.at[shard(d), :], give_send.at[d], give_recv.at[d], device(dp, z, r ^ 1)
         )
@@ -395,12 +397,21 @@
         remote(here, here, sum_send.at[i, s, p], sum_recv.at[i, s, p], device(dp, z, r ^ 1)).wait_recv()
         return here[...].astype(F32)
 
+    def far_gift(i, h):
+        return remote(
+            give_vm.at[piece(4, h), :], extra_vm.at[i], extra_send.at[i], extra_recv.at[i],
+            device(dp, z + (1 - 2 * i), r ^ 1),
+        )
+
     combine(4)
+    pass_on(0, 0, 0, own_vm[piece(4, 0), :])
+    pass_on(1, 0, 1, own_vm[piece(4, 1), :])
+    for i in range(2):
+        copy = far_gift(i, i)
+        copy.start()
+        sends.append(copy)
     combine(3)
     combine(5)
-    ready(4)
-    pass_on(0, 0, 0, total(4, 0))
-    pass_on(1, 0, 1, total(4, 1))
     ready(3)
     ready(5)
     pass_on(0, 1, 1, total(3, 1))
@@ -410,8 +421,10 @@
     query_terms((1 - r // 2) * 2)
     send_back(2)
     send_back(3)
-    pass_on(0, 1, 0, total(3, 0) + came(0, 0, 0))
-    pass_on(1, 1, 1, total(5, 1) + came(1, 0, 1))
+    for i, d in ((0, 3), (1, 5)):
+        value = total(d, i) + came(i, 0, i)
+        far_gift(i, i).wait_recv()
+        pass_on(i, 1, i, value + extra_vm[i].astype(F32))
     ready(2)
     ready(6)
     for h in range(2):
@@ -473,7 +486,7 @@
             remote(here, here, last_send.at[2, p], last_recv.at[2, p], device(dp, z, r ^ 1)).wait_send()
     for copy in sends:
         copy.wait_send()
-    for d in order:
+    for d in order[1:]:
         gifts[d].wait_send()
     for copy in heads:
         copy.wait()
@@ -516,6 +529,7 @@
             pltpu.VMEM((SEQ, HD), F32),
             pltpu.VMEM((SEQ, HD), BF16),
             pltpu.VMEM((SEQ, HD), BF16),
+            pltpu.VMEM((2, 2 * ROWS, HD), BF16),
             pltpu.VMEM((2, 3, 2, 2 * ROWS, HD), BF16),
             pltpu.VMEM((2, 3, 2, 2 * ROWS, HD), BF16),
             pltpu.VMEM((3, QUAD, ROWS, HD), BF16),
@@ -534,6 +548,8 @@
             DMA((3,)),
             DMA((RING,)),
             DMA((RING,)),
+            DMA((2,)),
+            DMA((2,)),
             DMA((2, 3, 2)),
             DMA((2, 3, 2)),
             DMA((3, QUAD)),

time: 60.5 us -> 59.3 us (0.980)
  Pallas kernels: 57.1 us -> 56 us
    pallas_call x1, Pallas kernels: 57.1 us -> 56 us  [local(): pl.pallas_call(kernel, out_shape=(jax.ShapeDtypeStruct((ROWS, HEADS * HD)...]
where the time goes in v4:
time: 59.3 us; the launch traced here: 59.2 us
  Pallas kernels  56 us (94%)
  other arithmetic  2.57 us (4%)
  between operations  0.66 us (1%)
    pallas_call x1, Pallas kernels, local(): pl.pallas_call(kernel, out_shape=(jax.ShapeDtypeStruct((ROWS, HEADS * HD)...  56 us
    mul x2, other arithmetic, local(): return tuple((half * 2 for half in halves))  2.57 us

profile of v4, /device:TPU:1, one launch (start us, length us, event | category | flops | bytes accessed | tf_op | source)
XLA Modules:
  0.0 59.2 jit_solution(7674275087153905975)
XLA Ops:
  0.6 56.0 %shard_map.103 = (bf16[128,2048]{1,0:T(8,128)(2,1)}, bf16[128,256]{1,0:T(8,128)(2,1)}, bf16[128,256]{1,0:T(8,128)(2,1)}) custom-call(bf16[128,2048]{1,0:T(8,128)(2,1)} %q_ref.1, bf16[128,256]{1,0:T(8,128)(2,1)} %k_ref.1, bf16[128,256]{1,0:T(8,128)(2,1)} %v_ref.1, bf16[128,2048]{1,0:T(8,128)(2,1)} %o_ref.1, bf16[128,2048]{1,0:T(8,128)(2,1)} %do_ref.1, ...), custom_call_target="tpu_custom_call" | custom-call | tf_op jit(solution)/shard_map/pallas_call | solution.py:502
  56.6 0.0 copy-start
  56.6 0.0 copy-start.1
  56.6 1.9 %broadcast_multiply_fusion = bf16[128,2048]{1,0:T(8,128)(2,1)} fusion(bf16[128,2048]{1,0:T(8,128)(2,1)} %get-tuple-element.6), kind=kLoop, calls=%fused_computation | loop fusion | flops 262144 | bytes 1048576 | tf_op jit(solution)/shard_map/mul | solution.py:565
  58.5 0.0 copy-done
  58.5 0.0 copy-done.1
  58.5 0.7 %broadcast_multiply_fusion.1 = (bf16[128,256]{1,0:T(8,128)(2,1)}, bf16[128,256]{1,0:T(8,128)(2,1)}) fusion(bf16[128,256]{1,0:T(8,128)(2,1)S(1)} %copy-done.1, bf16[128,256]{1,0:T(8,128)(2,1)S(1)} %copy-done), kind=kLoop, calls=%fused_computation.1 | loop fusion | flops 65536 | bytes 262144 | tf_op jit(solution)/shard_map/mul | solution.py:565
Async XLA Ops:
  56.6 1.9 %copy-start = (bf16[128,256]{1,0:T(8,128)(2,1)S(1)}, bf16[128,256]{1,0:T(8,128)(2,1)}, u32[]{:S(2)}) copy-start(bf16[128,256]{1,0:T(8,128)(2,1)} %get-tuple-element.7) | copy-start | bytes 196612
  56.6 1.9 %copy-start.1 = (bf16[128,256]{1,0:T(8,128)(2,1)S(1)}, bf16[128,256]{1,0:T(8,128)(2,1)}, u32[]{:S(2)}) copy-start(bf16[128,256]{1,0:T(8,128)(2,1)} %get-tuple-element.8) | copy-start | bytes 196612

commit v5 on v4

--- a/solution.py
+++ b/solution.py
@@ -331,7 +331,7 @@
     def combine(d):
         start = lax.rem(z + d + RING, RING) * BLOCKS_HERE
 
-        @pl.loop(0, BLOCKS_HERE, unroll=2)
+        @pl.loop(0, BLOCKS_HERE, unroll=4)
         def _(i):
             kb = order_sm[start + i]
             places = []

time: 59.3 us -> 59.3 us (level)
  no operation moved by 1% of the time
where the time goes in v5:
time: 59.3 us; the launch traced here: 59.2 us
  Pallas kernels  56 us (94%)
  other arithmetic  2.57 us (4%)
  between operations  0.66 us (1%)
    pallas_call x1, Pallas kernels, local(): pl.pallas_call(kernel, out_shape=(jax.ShapeDtypeStruct((ROWS, HEADS * HD)...  56 us
    mul x2, other arithmetic, local(): return tuple((half * 2 for half in halves))  2.57 us

profile of v5, /device:TPU:1, one launch (start us, length us, event | category | flops | bytes accessed | tf_op | source)
XLA Modules:
  0.0 59.2 jit_solution(6443696016605765587)
XLA Ops:
  0.6 56.0 %shard_map.103 = (bf16[128,2048]{1,0:T(8,128)(2,1)}, bf16[128,256]{1,0:T(8,128)(2,1)}, bf16[128,256]{1,0:T(8,128)(2,1)}) custom-call(bf16[128,2048]{1,0:T(8,128)(2,1)} %q_ref.1, bf16[128,256]{1,0:T(8,128)(2,1)} %k_ref.1, bf16[128,256]{1,0:T(8,128)(2,1)} %v_ref.1, bf16[128,2048]{1,0:T(8,128)(2,1)} %o_ref.1, bf16[128,2048]{1,0:T(8,128)(2,1)} %do_ref.1, ...), custom_call_target="tpu_custom_call" | custom-call | tf_op jit(solution)/shard_map/pallas_call | solution.py:502
  56.6 0.0 copy-start
  56.6 0.0 copy-start.1
  56.6 1.9 %broadcast_multiply_fusion = bf16[128,2048]{1,0:T(8,128)(2,1)} fusion(bf16[128,2048]{1,0:T(8,128)(2,1)} %get-tuple-element.6), kind=kLoop, calls=%fused_computation | loop fusion | flops 262144 | bytes 1048576 | tf_op jit(solution)/shard_map/mul | solution.py:565
  58.5 0.0 copy-done
  58.5 0.0 copy-done.1
  58.5 0.7 %broadcast_multiply_fusion.1 = (bf16[128,256]{1,0:T(8,128)(2,1)}, bf16[128,256]{1,0:T(8,128)(2,1)}) fusion(bf16[128,256]{1,0:T(8,128)(2,1)S(1)} %copy-done.1, bf16[128,256]{1,0:T(8,128)(2,1)S(1)} %copy-done), kind=kLoop, calls=%fused_computation.1 | loop fusion | flops 65536 | bytes 262144 | tf_op jit(solution)/shard_map/mul | solution.py:565
Async XLA Ops:
  56.6 1.9 %copy-start = (bf16[128,256]{1,0:T(8,128)(2,1)S(1)}, bf16[128,256]{1,0:T(8,128)(2,1)}, u32[]{:S(2)}) copy-start(bf16[128,256]{1,0:T(8,128)(2,1)} %get-tuple-element.7) | copy-start | bytes 196612
  56.6 1.9 %copy-start.1 = (bf16[128,256]{1,0:T(8,128)(2,1)S(1)}, bf16[128,256]{1,0:T(8,128)(2,1)}, u32[]{:S(2)}) copy-start(bf16[128,256]{1,0:T(8,128)(2,1)} %get-tuple-element.8) | copy-start | bytes 196612
